TPU v7x, 32 devices: a whole 2x2x4 slice. The times are simulated.
32 devices in a mesh: asset: 2 (over y), earn: 4 (over x, core), age: 4 (over z).
Axes of the slice: x: 2, y: 2, z: 4, core: 2. Of those that a mesh axis runs over, the one named last changes fastest.
Arguments:
- values: float32 [8, 32, 512, 512], P('age', 'earn', 'asset'), may hold values from -6 to 6
- utility: float32 [8, 32, 512, 512], P('age', 'earn', 'asset'), may hold values from -6 to 6
- earn_prob: float32 [5, 32], P(None, 'earn'), may hold values from 0.1 to 1
- support_start: int32 [32], P('earn'), may hold values from 0 to 27, as said below
- liquid_offset: int32 [32, 512], P('earn'), may hold values from 0 to 508
- liquid_weight: float32 [4, 32, 512], P(None, 'earn'), may hold values from 0.05 to 0.45
- illiquid_offset: int32 [32, 512], P('earn'), may hold values from 0 to 508
- illiquid_weight: float32 [4, 32, 512], P(None, 'earn'), may hold values from 0.05 to 0.45
Outputs:
- updated: float32 [8, 32, 512, 512], P('age', 'earn', 'asset')
Inputs may be any that keep to these rules, and one draw needn't show every extreme that they name: support_start[e] lies between e - 4 and e, and support_start[e] + 4 is a valid state.
All inputs are finite; a program needn't handle non-finite values.
Results may differ from a plain program's by a relative error of at most 0.00005.
Values sent between devices are 32-bit elements; how exact they have to be, the bound alone decides.
A program may use at most 128 MiB of HBM per device.

v0:
```python
import jax
import jax.numpy as jnp
from jax import lax
from jax.sharding import PartitionSpec as P

REACH = 4
BAND = 4
ITERS = 2


DISCOUNT = 0.96
PRECISE = lax.Precision.HIGHEST


def extended(cells, sides, width):
    for axis, dim in sides:
        count = lax.axis_size(axis)
        ends = count - 1
        head = lax.slice_in_dim(cells, 0, width, axis=dim)
        tail = lax.slice_in_dim(cells, cells.shape[dim] - width, cells.shape[dim], axis=dim)
        cells = jnp.concatenate(
            [
                lax.ppermute(tail, axis, [(i, (i + 1) % count) for i in range(ends)]),
                cells,
                lax.ppermute(head, axis, [((i + 1) % count, i) for i in range(ends)]),
            ],
            axis=dim,
        )
    return cells


def passed_along(value, axis, by):
    count = lax.axis_size(axis)
    pairs = [(i, i + by) for i in range(count) if 0 <= i + by < count]
    return lax.ppermute(value, axis, pairs)


def band_matrix(offset, weight):
    extent = offset.shape[1]
    positions = jnp.arange(extent, dtype=jnp.int32)
    matrix = jnp.zeros((offset.shape[0], extent, extent), jnp.float32)
    for number in range(BAND):
        matrix = matrix + jnp.where(
            positions[None, None, :] == (offset + number)[:, :, None],
            weight[number][:, :, None],
            0.0,
        )
    return matrix


def expectation(stacked, earn_prob, support_start):
    padded = extended(stacked, (("earn", 1),), REACH)
    states_here = stacked.shape[1]
    first_state = lax.axis_index("earn") * states_here
    slots = jnp.arange(states_here + 2 * REACH, dtype=jnp.int32)
    prob_sum = jnp.sum(earn_prob, axis=0)
    mixing = jnp.zeros((states_here, states_here + 2 * REACH), jnp.float32)
    for number in range(REACH + 1):
        target = support_start + number - first_state + REACH
        mixing = mixing + jnp.where(
            slots[None, :] == target[:, None], (earn_prob[number] / prob_sum)[:, None], 0.0
        )
    return jnp.einsum("ij,tjxy->tixy", mixing, padded, precision=PRECISE)


def continuation(current, earn_prob, support_start):
    arrived = passed_along(current[:1], "age", -1)
    return expectation(jnp.concatenate([current[1:], arrived], axis=0), earn_prob, support_start)


def to_columns(stacked, finish):
    return finish(lax.all_to_all(stacked, "asset", split_axis=3, concat_axis=2, tiled=True))


def to_rows(stacked, finish):
    return finish(lax.all_to_all(stacked, "asset", split_axis=3, concat_axis=2, tiled=True))


def swap_inner(stacked):
    return jnp.swapaxes(stacked, 2, 3)


def local(
    values,
    utility,
    earn_prob,
    support_start,
    liquid_offset,
    liquid_weight,
    illiquid_offset,
    illiquid_weight,
):
    liquid_map = band_matrix(liquid_offset, liquid_weight)
    illiquid_map = band_matrix(illiquid_offset, illiquid_weight)

    def liquid_arrived(stacked):
        return jnp.einsum("eac,tecy->teya", liquid_map, stacked, precision=PRECISE)

    def illiquid_arrived(stacked):
        return jnp.einsum("ebc,tecx->texb", illiquid_map, stacked, precision=PRECISE)

    current = values
    utility_columns = to_columns(utility, swap_inner)
    for iteration in range(ITERS):
        expected = continuation(current, earn_prob, support_start)
        if iteration % 2 == 0:
            current = utility_columns + DISCOUNT * to_columns(
                jnp.einsum("eac,tebc->teba", liquid_map, expected, precision=PRECISE),
                illiquid_arrived,
            )
        else:
            current = utility + DISCOUNT * to_rows(
                jnp.einsum("ebc,texc->texb", illiquid_map, expected, precision=PRECISE),
                liquid_arrived,
            )
    return current


def solution(mesh):
    return jax.shard_map(
        local,
        mesh=mesh,
        in_specs=(
            P("age", "earn", "asset", None),
            P("age", "earn", "asset", None),
            P(None, "earn"),
            P("earn"),
            P("earn", None),
            P(None, "earn", None),
            P("earn", None),
            P(None, "earn", None),
        ),
        out_specs=P("age", "earn", "asset", None),
        check_vma=False,
    )
```

profile of v0, /device:TPU:17, one launch (start us, length us, event | category | flops | bytes accessed | tf_op | source)
XLA Modules:
  0.0 690.3 jit_solution(11076904609429193501)
XLA Ops:
  6.6 91.2 %collective-permute-done = f32[1,8,256,512]{3,2,1,0:T(8,128)S(1)} collective-permute-done((f32[1,8,256,512]{3,2,1,0:T(8,128)S(1)}, f32[1,8,256,512]{3,2,1,0:T(8,128)S(1)}, u32[]{:S(2)}, u32[]{:S(2)}) %collective-permute-start) | collective-permute-done | bytes 4194336 | tf_op jit(solution)/shard_map/ppermute | solution.py:35
  109.7 10.2 %copy.14 = f32[2,8,256,512]{2,1,0,3:T(8,128)} copy(f32[2,8,256,512]{3,2,1,0:T(8,128)} %param.9) | data formatting | bytes 16777216 | tf_op args[1]
  119.9 7.6 %all-to-all-start = ((f32[2,8,256,512]{2,1,0,3:T(8,128)}), f32[2,8,256,512]{2,1,0,3:T(8,128)}, u32[]{:S(2)}, u32[]{:S(2)}) async-start(f32[2,8,256,512]{2,1,0,3:T(8,128)} %copy.14), calls=%async_computation | async-start | bytes 16777216 | tf_op jit(solution)/shard_map/all_to_all | solution.py:72
  132.2 21.0 %collective-permute-done.1 = f32[2,4,256,512]{3,2,1,0:T(8,128)} collective-permute-done((f32[2,4,256,512]{3,2,1,0:T(8,128)}, f32[2,4,256,512]{3,2,1,0:T(8,128)}, u32[]{:S(2)}, u32[]{:S(2)}) %collective-permute-start.1) | collective-permute-done | bytes 4194336 | tf_op jit(solution)/shard_map/ppermute | solution.py:23
  163.8 17.5 %fusion.2 = f32[2,256,512,8]{2,3,1,0:T(8,128)} fusion(f32[2,16,256,512]{3,2,1,0:T(8,128)S(1)} %pad_maximum_fusion, f32[8]{0:T(128)S(1)} %get-tuple-element.28, s32[8]{0:T(128)S(1)} %get-tuple-element.35, f32[8]{0:T(128)S(1)} %get-tuple-element.29, s32[8]{0:T(128)S(1)} %get-tuple-element.36, f32[8]{0:T(128)S(1)} %get-tuple-element.30, ...), kind=kOutput, calls=%fused_computation.4 | convolution fusion | flops 402654976 | bytes 25166144 | tf_op jit(solution)/shard_map/ij,tjxy->tixy/dot_general | solution.py:63
  181.3 44.6 %fusion.54 = f32[2,8,256,512]{3,2,0,1:T(8,128)} fusion(f32[2,256,512,8]{2,3,1,0:T(8,128)} %fusion.2, f32[8,512,512,1]{2,1,3,0:T(8,128)S(1)} %fusion.115), kind=kOutput, calls=%fused_computation.77 | convolution fusion | flops 12884901888 | bytes 25165824 | tf_op jit(solution)/shard_map/eac,tebc->teba/dot_general | solution.py:108
  225.9 13.2 %copy.16 = f32[2,8,256,512]{2,0,1,3:T(2,128)} copy(f32[2,8,256,512]{3,2,0,1:T(8,128)} %fusion.54) | data formatting | bytes 16777216 | tf_op jit(solution)/shard_map/eac,tebc->teba/transpose | solution.py:108
  239.2 7.1 %all-to-all-start.1 = ((f32[2,8,256,512]{2,0,1,3:T(2,128)}), f32[2,8,256,512]{2,0,1,3:T(2,128)}, u32[]{:S(2)}, u32[]{:S(2)}) async-start(f32[2,8,256,512]{2,0,1,3:T(2,128)} %copy.16), calls=%async_computation.1 | async-start | bytes 16777216 | tf_op jit(solution)/shard_map/all_to_all | solution.py:72
  253.1 15.4 %copy.53 = f32[2,8,256,2,256]{2,3,4,0,1:T(2,128)} copy(f32[2,8,256,2,256]{2,1,0,4,3:T(8,128)} %bitcast) | data formatting | bytes 16777216 | tf_op jit(solution)/shard_map/all_to_all | solution.py:72
  268.5 11.6 %all_to_all.42 = f32[2,8,512,256]{2,3,0,1:T(8,128)} reshape(f32[2,8,2,256,256]{3,2,4,0,1:T(2,128)} %bitcast.116) | data formatting | bytes 16777216 | tf_op jit(solution)/shard_map/all_to_all | solution.py:72
  280.1 40.4 %all-to-all-done.1 = f32[2,8,256,512]{2,0,1,3:T(2,128)} async-done(((f32[2,8,256,512]{2,0,1,3:T(2,128)}), f32[2,8,256,512]{2,0,1,3:T(2,128)}, u32[]{:S(2)}, u32[]{:S(2)}) %all-to-all-start.1) | async-done | bytes 8388640 | tf_op jit(solution)/shard_map/all_to_all | solution.py:72
  320.5 15.3 %copy.52 = f32[2,8,256,2,256]{2,3,4,0,1:T(2,128)} copy(f32[2,8,256,2,256]{2,0,1,4,3:T(2,128)} %bitcast.18) | data formatting | bytes 16777216 | tf_op jit(solution)/shard_map/all_to_all | solution.py:72
  335.8 11.5 %all_to_all.46 = f32[2,8,512,256]{2,3,0,1:T(8,128)} reshape(f32[2,8,2,256,256]{3,2,4,0,1:T(2,128)} %bitcast.117) | data formatting | bytes 16777216 | tf_op jit(solution)/shard_map/all_to_all | solution.py:72
  347.3 20.0 %bitcast_add_fusion.1 = f32[2,8,256,512]{3,2,0,1:T(8,128)S(1)} fusion(f32[2,8,512,256]{2,3,0,1:T(8,128)} %all_to_all.42, f32[2,8,512,256]{2,3,0,1:T(8,128)} %all_to_all.46, f32[8,512,512,1]{2,1,3,0:T(8,128)} %fusion.113), kind=kOutput, calls=%fused_computation.20 | convolution fusion | flops 12889096192 | bytes 33554432 | tf_op jit(solution)/shard_map/ebc,tecx->texb/dot_general | solution.py:100
  370.7 74.8 %collective-permute-done.3 = f32[1,8,256,512]{3,2,0,1:T(8,128)S(1)} collective-permute-done((f32[1,8,256,512]{3,2,0,1:T(8,128)S(1)}, f32[1,8,256,512]{3,2,0,1:T(8,128)S(1)}, u32[]{:S(2)}, u32[]{:S(2)}) %collective-permute-start.3) | collective-permute-done | bytes 4194336 | tf_op jit(solution)/shard_map/ppermute | solution.py:35
  452.2 7.1 %fusion.117 = f32[8,512,512,1]{2,1,3,0:T(8,128)} fusion(f32[8,512]{1,0:T(8,128)S(1)} %get-tuple-element.19, s32[8,512]{1,0:T(8,128)S(1)} %get-tuple-element.25, f32[8,512]{1,0:T(8,128)S(1)} %get-tuple-element.20, s32[8,512]{1,0:T(8,128)S(1)} %get-tuple-element.26, f32[8,512]{1,0:T(8,128)S(1)} %get-tuple-element.18, ...), kind=kLoop, calls=%fused_computation.11.clone.clone.clone | loop fusion | flops 23068672 | bytes 8519680 | tf_op jit(solution)/shard_map/ebc,texc->texb/dot_general | solution.py:113
  459.4 36.3 %collective-permute-done.4 = f32[2,4,256,512]{3,2,0,1:T(8,128)S(1)} collective-permute-done((f32[2,4,256,512]{3,2,0,1:T(8,128)S(1)}, f32[2,4,256,512]{3,2,0,1:T(8,128)S(1)}, u32[]{:S(2)}, u32[]{:S(2)}) %collective-permute-start.4) | collective-permute-done | bytes 4194336 | tf_op jit(solution)/shard_map/ppermute | solution.py:23
  504.6 17.5 %fusion = f32[2,256,512,8]{2,3,1,0:T(8,128)} fusion(f32[2,16,256,512]{3,2,0,1:T(8,128)S(1)} %pad_maximum_fusion.1, f32[8]{0:T(128)S(1)} %get-tuple-element.28, s32[8]{0:T(128)S(1)} %get-tuple-element.35, f32[8]{0:T(128)S(1)} %get-tuple-element.29, s32[8]{0:T(128)S(1)} %get-tuple-element.36, f32[8]{0:T(128)S(1)} %get-tuple-element.30, ...), kind=kOutput, calls=%fused_computation.2 | convolution fusion | flops 402654976 | bytes 25166144 | tf_op jit(solution)/shard_map/ij,tjxy->tixy/dot_general | solution.py:63
  522.1 44.6 %fusion.59 = f32[2,8,256,512]{3,2,0,1:T(8,128)} fusion(f32[2,256,512,8]{2,3,1,0:T(8,128)} %fusion, f32[8,512,512,1]{2,1,3,0:T(8,128)S(1)} %copy-done.2), kind=kOutput, calls=%fused_computation.78 | convolution fusion | flops 12884901888 | bytes 25165824 | tf_op jit(solution)/shard_map/ebc,texc->texb/dot_general | solution.py:113
  566.7 13.1 %copy.18 = f32[2,8,256,512]{2,0,1,3:T(2,128)} copy(f32[2,8,256,512]{3,2,0,1:T(8,128)} %fusion.59) | data formatting | bytes 16777216 | tf_op jit(solution)/shard_map/ebc,texc->texb/transpose | solution.py:113
  593.8 45.4 %all-to-all-done.2 = f32[2,8,256,512]{2,0,1,3:T(2,128)} async-done(((f32[2,8,256,512]{2,0,1,3:T(2,128)}), f32[2,8,256,512]{2,0,1,3:T(2,128)}, u32[]{:S(2)}, u32[]{:S(2)}) %all-to-all-start.2) | async-done | bytes 8388640 | tf_op jit(solution)/shard_map/all_to_all | solution.py:76
  639.2 15.3 %copy.51 = f32[2,8,256,2,256]{2,3,4,0,1:T(2,128)} copy(f32[2,8,256,2,256]{2,0,1,4,3:T(2,128)} %bitcast.29) | data formatting | bytes 16777216 | tf_op jit(solution)/shard_map/all_to_all | solution.py:76
  654.5 11.5 %all_to_all.50 = f32[2,8,512,256]{2,3,0,1:T(8,128)} reshape(f32[2,8,2,256,256]{3,2,4,0,1:T(2,128)} %bitcast.118) | data formatting | bytes 16777216 | tf_op jit(solution)/shard_map/all_to_all | solution.py:76
  665.9 19.8 %bitcast_add_fusion = f32[2,8,256,512]{3,2,0,1:T(8,128)S(1)} fusion(f32[2,8,256,512]{3,2,1,0:T(8,128)} %param.9, f32[2,8,512,256]{2,3,0,1:T(8,128)} %all_to_all.50, f32[8,512,512,1]{2,1,3,0:T(8,128)} %fusion.111), kind=kOutput, calls=%fused_computation.18 | convolution fusion | flops 12889096192 | bytes 33554432 | tf_op jit(solution)/shard_map/eac,tecy->teya/dot_general | solution.py:97
  (47 shorter events, 77.6 us)
Async XLA Ops:
  4.5 97.8 %copy-start = (f32[1,8,256,512]{3,2,1,0:T(8,128)}, f32[1,8,256,512]{3,2,1,0:T(8,128)S(1)}, u32[]{:S(2)}) copy-start(f32[1,8,256,512]{3,2,1,0:T(8,128)S(1)} %get-tuple-element.11) | copy-start | bytes 12582916
  4.5 93.3 %collective-permute-start = (f32[1,8,256,512]{3,2,1,0:T(8,128)S(1)}, f32[1,8,256,512]{3,2,1,0:T(8,128)S(1)}, u32[]{:S(2)}, u32[]{:S(2)}) collective-permute-start(f32[1,8,256,512]{3,2,1,0:T(8,128)S(1)} %get-tuple-element.12), channel_id=1, source_target_pairs={{1,0},{2,1},{3,2},{5,4},{6,5},{7,6},{9,8},{10,9},{11,10},{13,12},{... | collective-permute-start | bytes 12582920 | tf_op jit(solution)/shard_map/ppermute | solution.py:35
  97.8 5.1 copy-start.3
  102.9 50.3 %collective-permute-start.1 = (f32[2,4,256,512]{3,2,1,0:T(8,128)}, f32[2,4,256,512]{3,2,1,0:T(8,128)}, u32[]{:S(2)}, u32[]{:S(2)}) collective-permute-start(f32[2,4,256,512]{3,2,1,0:T(8,128)} %get-tuple-element.9), channel_id=1, source_target_pairs={{0,4},{4,8},{8,12},{1,5},{5,9},{9,13},{2,6},{6,10},{10,14},{3,7},{... | collective-permute-start | bytes 12582920 | tf_op jit(solution)/shard_map/ppermute | solution.py:23
  107.4 50.4 %collective-permute-start.2 = (f32[2,4,256,512]{3,2,1,0:T(8,128)}, f32[2,4,256,512]{3,2,1,0:T(8,128)}, u32[]{:S(2)}, u32[]{:S(2)}) collective-permute-start(f32[2,4,256,512]{3,2,1,0:T(8,128)} %get-tuple-element.10), channel_id=1, source_target_pairs={{4,0},{8,4},{12,8},{5,1},{9,5},{13,9},{6,2},{10,6},{14,10},{7,3},{... | collective-permute-start | bytes 12582920 | tf_op jit(solution)/shard_map/ppermute | solution.py:25
  119.9 7.7 %copy-start.8 = (f32[5,8]{1,0:T(8,128)S(1)}, f32[5,8]{1,0:T(8,128)}, u32[]{:S(2)}) copy-start(f32[5,8]{1,0:T(8,128)} %param.10) | copy-start | bytes 484
  119.9 7.7 %copy-start.5 = (s32[8,512]{1,0:T(8,128)S(1)}, s32[8,512]{1,0:T(8,128)}, u32[]{:S(2)}) copy-start(s32[8,512]{1,0:T(8,128)} %param.12) | copy-start | bytes 49156
  119.9 7.7 %copy-start.9 = (s32[8]{0:T(128)S(1)}, s32[8]{0:T(128)}, u32[]{:S(2)}) copy-start(s32[8]{0:T(128)} %param.11) | copy-start | bytes 100
  119.9 7.8 %copy-start.6 = (f32[4,8,512]{2,1,0:T(8,128)S(1)}, f32[4,8,512]{2,1,0:T(8,128)}, u32[]{:S(2)}) copy-start(f32[4,8,512]{2,1,0:T(8,128)} %param.13) | copy-start | bytes 196612
  119.9 119.3 %all-to-all-start = ((f32[2,8,256,512]{2,1,0,3:T(8,128)}), f32[2,8,256,512]{2,1,0,3:T(8,128)}, u32[]{:S(2)}, u32[]{:S(2)}) async-start(f32[2,8,256,512]{2,1,0,3:T(8,128)} %copy.14), calls=%async_computation | async-start | bytes 16777216 | tf_op jit(solution)/shard_map/all_to_all | solution.py:72
  127.6 30.3 %copy-start.1 = (f32[1,8,256,512]{3,2,1,0:T(8,128)S(1)}, f32[1,8,256,512]{3,2,1,0:T(8,128)}, u32[]{:S(2)}) copy-start(f32[1,8,256,512]{3,2,1,0:T(8,128)} %copy-done) | copy-start | bytes 12582916
  239.2 7.1 %copy-start.4 = (s32[8,512]{1,0:T(8,128)S(1)}, s32[8,512]{1,0:T(8,128)}, u32[]{:S(2)}) copy-start(s32[8,512]{1,0:T(8,128)} %param.14) | copy-start | bytes 49156
  239.2 7.2 %copy-start.7 = (f32[4,8,512]{2,1,0:T(8,128)S(1)}, f32[4,8,512]{2,1,0:T(8,128)}, u32[]{:S(2)}) copy-start(f32[4,8,512]{2,1,0:T(8,128)} %param.15) | copy-start | bytes 196612
  239.2 81.3 %all-to-all-start.1 = ((f32[2,8,256,512]{2,0,1,3:T(2,128)}), f32[2,8,256,512]{2,0,1,3:T(2,128)}, u32[]{:S(2)}, u32[]{:S(2)}) async-start(f32[2,8,256,512]{2,0,1,3:T(2,128)} %copy.16), calls=%async_computation.1 | async-start | bytes 16777216 | tf_op jit(solution)/shard_map/all_to_all | solution.py:72
  368.7 76.9 %collective-permute-start.3 = (f32[1,8,256,512]{3,2,0,1:T(8,128)S(1)}, f32[1,8,256,512]{3,2,0,1:T(8,128)S(1)}, u32[]{:S(2)}, u32[]{:S(2)}) collective-permute-start(f32[1,8,256,512]{3,2,0,1:T(8,128)S(1)} %get-tuple-element.8), channel_id=1, source_target_pairs={{1,0},{2,1},{3,2},{5,4},{6,5},{7,6},{9,8},{10,9},{11,10},{13,12},{... | collective-permute-start | bytes 12582920 | tf_op jit(solution)/shard_map/ppermute | solution.py:35
  446.8 48.9 %collective-permute-start.4 = (f32[2,4,256,512]{3,2,0,1:T(8,128)S(1)}, f32[2,4,256,512]{3,2,0,1:T(8,128)S(1)}, u32[]{:S(2)}, u32[]{:S(2)}) collective-permute-start(f32[2,4,256,512]{3,2,0,1:T(8,128)S(1)} %get-tuple-element.5), channel_id=1, source_target_pairs={{0,4},{4,8},{8,12},{1,5},{5,9},{9,13},{2,6},{6,10},{10,14},{3,7},{... | collective-permute-start | bytes 12582920 | tf_op jit(solution)/shard_map/ppermute | solution.py:23
  450.3 49.9 %collective-permute-start.5 = (f32[2,4,256,512]{3,2,0,1:T(8,128)S(1)}, f32[2,4,256,512]{3,2,0,1:T(8,128)}, u32[]{:S(2)}, u32[]{:S(2)}) collective-permute-start(f32[2,4,256,512]{3,2,0,1:T(8,128)S(1)} %get-tuple-element.6), channel_id=1, source_target_pairs={{4,0},{8,4},{12,8},{5,1},{9,5},{13,9},{6,2},{10,6},{14,10},{7,3},{... | collective-permute-start | bytes 12582920 | tf_op jit(solution)/shard_map/ppermute | solution.py:25
  504.6 17.5 %copy-start.2 = (f32[8,512,512,1]{2,1,3,0:T(8,128)S(1)}, f32[8,512,512,1]{2,1,3,0:T(8,128)}, u32[]{:S(2)}) copy-start(f32[8,512,512,1]{2,1,3,0:T(8,128)} %fusion.117) | copy-start | bytes 25165828
  579.8 59.3 %all-to-all-start.2 = ((f32[2,8,256,512]{2,0,1,3:T(2,128)}), f32[2,8,256,512]{2,0,1,3:T(2,128)}, u32[]{:S(2)}, u32[]{:S(2)}) async-start(f32[2,8,256,512]{2,0,1,3:T(2,128)} %copy.18), calls=%async_computation.2 | async-start | bytes 16777216 | tf_op jit(solution)/shard_map/all_to_all | solution.py:76
where the time goes:
time: 696 us; the launch traced here: 690 us
  waiting for transfers between devices  318 us (46%)
  matrix products  164 us (24%)
  local copies, waits for them, and re-layouts  128 us (18%)
  other arithmetic  41.4 us (6%)
  starting transfers between devices  38 us (5%)
    ppermute x2, waiting for transfers between devices, passed_along(): return lax.ppermute(value, axis, pairs)  166 us
    ppermute x2, waiting for transfers between devices, extended(): lax.ppermute(tail, axis, [(i, (i + 1) % count) for i in range(ends)])  57.4 us
    all_to_all x4, local copies, waits for them, and re-layouts, to_columns(): lax.all_to_all(stacked, 'asset', split_axis=3, concat_axis=2, tiled=True)  53.8 us
    all_to_all x1, waiting for transfers between devices, to_rows(): lax.all_to_all(stacked, 'asset', split_axis=3, concat_axis=2, tiled=True)  45.4 us
    dot_general x1, matrix products, local(): jnp.einsum('ebc,texc->texb', illiquid_map, expected, precision=PRECISE)  44.6 us
    dot_general x1, matrix products, local(): jnp.einsum('eac,tebc->teba', liquid_map, expected, precision=PRECISE)  44.6 us
    all_to_all x2, waiting for transfers between devices, to_columns(): lax.all_to_all(stacked, 'asset', split_axis=3, concat_axis=2, tiled=True)  40.4 us
    dot_general x2, matrix products, expectation(): return jnp.einsum('ij,tjxy->tixy', mixing, padded, precision=PRECISE)  35 us
  transfers between devices with their start and end apart: 9, of which 8 were waited for; matrix products, arithmetic and copies ran while one was open for 19% of the time, Pallas kernels for 0%

commit v1 on v0

v1 whole, which is shorter than its diff:
```python
import functools

import jax
import jax.numpy as jnp
from jax import lax
from jax.experimental import pallas as pl
from jax.experimental.pallas import tpu as pltpu
from jax.sharding import PartitionSpec as P

REACH = 4
BAND = 4
DISCOUNT = 0.96
SPAN = 2 * REACH + 1
VMEM_BYTES = 48 * 1024 * 1024


def params():
    return pltpu.CompilerParams(vmem_limit_bytes=VMEM_BYTES)


def halves(x):
    high = x.astype(jnp.bfloat16)
    return high, (x - high.astype(jnp.float32)).astype(jnp.bfloat16)


def dot3(ah, al, bh, bl):
    dot = functools.partial(jnp.dot, preferred_element_type=jnp.float32)
    return dot(ah, bh) + (dot(ah, bl) + dot(al, bh))


def band_kernel(flip, bases, offset, weight, high, low, full):
    count = bases.shape[0]
    extent = full.shape[0]
    width = extent // count
    step = min(width, 32)
    first = offset[0]
    for block in range(count):
        for row in range(0, width, step):
            place = lax.broadcasted_iota(jnp.int32, (step, extent), 0) + (bases[block] + row)
            gap = place - first
            value = jnp.zeros((step, extent), jnp.float32)
            for number in range(BAND):
                value = jnp.where(gap == number, weight[number, 0], value)
            full[pl.ds(block * width + row, step), :] = value
    matrix = full[...]
    if flip:
        matrix = matrix.T
    high[0], low[0] = halves(matrix)


def band_pair(offset, weight, bases, flip):
    states, extent = offset.shape
    out = jax.ShapeDtypeStruct((states, extent, extent), jnp.bfloat16)
    spec = pl.BlockSpec((1, extent, extent), lambda e: (e, 0, 0))
    return pl.pallas_call(
        functools.partial(band_kernel, flip),
        grid=(states,),
        out_shape=(out, out),
        in_specs=[
            pl.BlockSpec(memory_space=pltpu.SMEM),
            pl.BlockSpec((1, 1, extent), lambda e: (e, 0, 0)),
            pl.BlockSpec((BAND, 1, 1, extent), lambda e: (0, e, 0, 0)),
        ],
        out_specs=(spec, spec),
        scratch_shapes=[pltpu.VMEM((extent, extent), jnp.float32)],
        compiler_params=params(),
        cost_estimate=pl.CostEstimate(
            flops=states * extent * extent * 12, bytes_accessed=states * extent * extent * 4, transcendentals=0
        ),
        name="band",
    )(bases, offset[:, None, :], weight[:, :, None, :])


def mix_kernel(base, left_product, pieces, mixing, below, here, above, high, low, *rest):
    outs, (slabs, xh, xl, sems) = rest[:pieces], rest[pieces:]
    e = pl.program_id(0)
    quad = here.shape[0]

    def fetch(source, group):
        return [
            pltpu.make_async_copy(source.at[i], slabs.at[group * quad + i], sems.at[group * quad + i])
            for i in range(quad)
        ]

    copies = fetch(below, 0) + fetch(here, 1) + fetch(above, 2)

    @pl.when(e == 0)
    def _():
        for copy in copies:
            copy.start()
        for copy in copies[: SPAN - 1]:
            copy.wait()

    for number in range(quad):

        @pl.when(e == number)
        def _():
            copies[number + SPAN - 1].wait()

    rows = xh.shape[0]
    step = 16
    shares = [mixing[base + e, d] for d in range(SPAN)]

    def chunk(i, carry):
        at = pl.ds(pl.multiple_of(i * step, step), step)
        total = shares[0] * slabs[e, at, :]
        for d in range(1, SPAN):
            total = total + shares[d] * slabs[e + d, at, :]
        xh[at, :], xl[at, :] = halves(total)
        return carry

    lax.fori_loop(0, rows // step, chunk, 0)
    if left_product:
        result = dot3(high[0], low[0], xh[...], xl[...])
        width = result.shape[0] // pieces
        for s in range(pieces):
            outs[s][0] = result[s * width : (s + 1) * width]
    else:
        result = dot3(xh[...], xl[...], high[0], low[0])
        width = result.shape[1] // pieces
        for s in range(pieces):
            outs[s][0] = result[:, s * width : (s + 1) * width]


def mixed_product(below, here, above, mixing, pair, base, left_product, pieces):
    quad, rows, columns = here.shape
    extent = pair[0].shape[1]
    shape = (rows // pieces, columns) if left_product else (rows, columns // pieces)
    matrix = pl.BlockSpec((1, extent, extent), lambda e: (base + e, 0, 0))
    return pl.pallas_call(
        functools.partial(mix_kernel, base, left_product, pieces),
        grid=(quad,),
        out_shape=[jax.ShapeDtypeStruct((quad,) + shape, jnp.float32)] * pieces,
        in_specs=[pl.BlockSpec(memory_space=pltpu.SMEM)]
        + [pl.BlockSpec(memory_space=pl.ANY)] * 3
        + [matrix] * 2,
        out_specs=[pl.BlockSpec((1,) + shape, lambda e: (e, 0, 0))] * pieces,
        scratch_shapes=[
            pltpu.VMEM((3 * quad, rows, columns), jnp.float32),
            pltpu.VMEM((rows, columns), jnp.bfloat16),
            pltpu.VMEM((rows, columns), jnp.bfloat16),
            pltpu.SemaphoreType.DMA((3 * quad,)),
        ],
        compiler_params=params(),
        cost_estimate=pl.CostEstimate(
            flops=quad * rows * columns * extent * 6,
            bytes_accessed=4 * quad * rows * columns * 4 + 4 * quad * extent * extent,
            transcendentals=0,
        ),
        name="mix_band",
    )(mixing, below, here, above, *pair)


def column_kernel(pieces, high, low, *rest):
    parts, flows, (out, xh, xl) = rest[:pieces], rest[pieces : 2 * pieces], rest[2 * pieces :]
    rows = parts[0].shape[1]
    for s in range(pieces):
        at = pl.ds(s * rows, rows)
        xh[at, :], xl[at, :] = halves(parts[s][0])
    result = dot3(high[0], low[0], xh[...], xl[...])
    for s in range(pieces):
        at = pl.ds(s * rows, rows)
        out[0, at, :] = flows[s][0] + DISCOUNT * result[s * rows : (s + 1) * rows]


def column_product(parts, flows, pair, base):
    pieces = len(parts)
    quad, rows, columns = parts[0].shape
    extent = pair[0].shape[1]
    matrix = pl.BlockSpec((1, extent, extent), lambda e: (base + e, 0, 0))
    piece = pl.BlockSpec((1, rows, columns), lambda e: (e, 0, 0))
    flow = pl.BlockSpec((1, rows, columns), lambda e: (base + e, 0, 0))
    return pl.pallas_call(
        functools.partial(column_kernel, pieces),
        grid=(quad,),
        out_shape=jax.ShapeDtypeStruct((quad, extent, columns), jnp.float32),
        in_specs=[matrix] * 2 + [piece] * pieces + [flow] * pieces,
        out_specs=pl.BlockSpec((1, extent, columns), lambda e: (e, 0, 0)),
        scratch_shapes=[pltpu.VMEM((extent, columns), jnp.bfloat16)] * 2,
        compiler_params=params(),
        cost_estimate=pl.CostEstimate(
            flops=quad * extent * columns * extent * 6,
            bytes_accessed=3 * quad * extent * columns * 4 + 4 * quad * extent * extent,
            transcendentals=0,
        ),
        name="columns_band",
    )(*pair, *parts, *flows)


def row_product_of(parts, high, low):
    width = parts[0].shape[2]
    result = None
    for s, part in enumerate(parts):
        xh, xl = halves(part[0])
        at = pl.ds(s * width, width)
        term = dot3(xh, xl, high[0, at, :], low[0, at, :])
        result = term if result is None else result + term
    return result


def row_kernel(pieces, high, low, *rest):
    parts, out = rest[:pieces], rest[pieces]
    out[0] = row_product_of(parts, high, low)


def row_product(parts, pair, base):
    pieces = len(parts)
    quad, rows, columns = parts[0].shape
    extent = pair[0].shape[1]
    matrix = pl.BlockSpec((1, extent, extent), lambda e: (base + e, 0, 0))
    piece = pl.BlockSpec((1, rows, columns), lambda e: (e, 0, 0))
    return pl.pallas_call(
        functools.partial(row_kernel, pieces),
        grid=(quad,),
        out_shape=jax.ShapeDtypeStruct((quad, rows, extent), jnp.float32),
        in_specs=[matrix] * 2 + [piece] * pieces,
        out_specs=pl.BlockSpec((1, rows, extent), lambda e: (e, 0, 0)),
        compiler_params=params(),
        cost_estimate=pl.CostEstimate(
            flops=quad * rows * extent * extent * 6,
            bytes_accessed=2 * quad * rows * extent * 4 + 4 * quad * extent * extent,
            transcendentals=0,
        ),
        name="rows_band",
    )(*pair, *parts)


def last_row_kernel(pieces, high, low, flow, *rest):
    parts, out = rest[:pieces], rest[-1]
    out[0, 0] = flow[0, 0] + DISCOUNT * row_product_of(parts, high, low)


def last_rows(parts, pair, base, utility, age, whole):
    pieces = len(parts)
    quad, rows, columns = parts[0].shape
    extent = pair[0].shape[1]
    matrix = pl.BlockSpec((1, extent, extent), lambda e: (base + e, 0, 0))
    piece = pl.BlockSpec((1, rows, columns), lambda e: (e, 0, 0))
    flow = pl.BlockSpec((1, 1, rows, extent), lambda e: (age, base + e, 0, 0))
    return pl.pallas_call(
        functools.partial(last_row_kernel, pieces),
        grid=(quad,),
        out_shape=jax.ShapeDtypeStruct(utility.shape, jnp.float32),
        in_specs=[matrix] * 2 + [flow] + [piece] * pieces + [pl.BlockSpec(memory_space=pl.ANY)],
        out_specs=flow,
        input_output_aliases={3 + pieces: 0},
        compiler_params=params(),
        cost_estimate=pl.CostEstimate(
            flops=quad * rows * extent * extent * 6,
            bytes_accessed=3 * quad * rows * extent * 4 + 4 * quad * extent * extent,
            transcendentals=0,
        ),
        name="last_rows",
    )(*pair, utility, *parts, whole)


def add_kernel(flow, arrived, *rest):
    rest[-1][0, 0] = flow[0, 0] + DISCOUNT * arrived[0]


def last_sum(arrived, base, utility, age, whole):
    quad, rows, extent = arrived.shape
    flow = pl.BlockSpec((1, 1, rows, extent), lambda e: (age, base + e, 0, 0))
    part = pl.BlockSpec((1, rows, extent), lambda e: (e, 0, 0))
    before = () if whole is None else (whole,)
    return pl.pallas_call(
        add_kernel,
        grid=(quad,),
        out_shape=jax.ShapeDtypeStruct(utility.shape, jnp.float32),
        in_specs=[flow, part] + [pl.BlockSpec(memory_space=pl.ANY)] * len(before),
        out_specs=flow,
        input_output_aliases={} if whole is None else {2: 0},
        compiler_params=params(),
        cost_estimate=pl.CostEstimate(
            flops=quad * rows * extent * 2, bytes_accessed=3 * quad * rows * extent * 4, transcendentals=0
        ),
        name="last_sum",
    )(utility, arrived, *before)


def shifted(value, axis, by):
    count = lax.axis_size(axis)
    return lax.ppermute(value, axis, [(i, i + by) for i in range(count) if 0 <= i + by < count])


def exchanged(pieces):
    count = lax.axis_size("asset")
    return [pieces[0]] + [
        lax.ppermute(pieces[s], "asset", [(i, (i + s) % count) for i in range(count)])
        for s in range(1, count)
    ]


def local(
    values,
    utility,
    earn_prob,
    support_start,
    liquid_offset,
    liquid_weight,
    illiquid_offset,
    illiquid_weight,
):
    count = lax.axis_size("asset")
    me = lax.axis_index("asset")
    states = values.shape[1]
    quad = REACH
    assert states == 2 * quad
    rows = values.shape[2]
    columns = values.shape[3] // count

    ahead = [(me + s) % count for s in range(count)]
    behind = [(me - s + count) % count for s in range(count)]

    def in_blocks(x, blocks, width):
        return jnp.concatenate(
            [lax.dynamic_slice_in_dim(x, block * width, width, axis=x.ndim - 1) for block in blocks], axis=-1
        )

    def starts(blocks, width):
        return jnp.stack([jnp.asarray(block * width, jnp.int32) for block in blocks])

    natural_columns = starts(range(count), columns)
    behind_columns = starts(behind, columns)
    behind_rows = starts(behind, rows)

    liquid_first = band_pair(
        in_blocks(liquid_offset, ahead, columns), in_blocks(liquid_weight, ahead, columns), natural_columns, False
    )
    illiquid_first = band_pair(
        in_blocks(illiquid_offset, behind, rows), in_blocks(illiquid_weight, behind, rows), behind_rows, True
    )
    if count == 2:
        illiquid_second = illiquid_first
    else:
        illiquid_second = band_pair(
            in_blocks(illiquid_offset, ahead, rows), in_blocks(illiquid_weight, ahead, rows), behind_rows, True
        )
    liquid_second = band_pair(liquid_offset, liquid_weight, behind_columns, False)

    shares = earn_prob / jnp.sum(earn_prob, axis=0, keepdims=True)
    own = lax.axis_index("earn") * states + jnp.arange(states, dtype=jnp.int32)
    slots = jnp.arange(SPAN, dtype=jnp.int32)
    mixing = jnp.zeros((states, SPAN), jnp.float32)
    for number in range(REACH + 1):
        slot = support_start + number - own + REACH
        mixing = mixing + jnp.where(slots[None, :] == slot[:, None], shares[number][:, None], 0.0)

    def with_sides(head, tail):
        return [shifted(tail, "earn", 1), head, tail, shifted(head, "earn", -1)]

    def first_half(head, tail):
        quads = with_sides(head, tail)
        return [
            exchanged(mixed_product(*quads[i : i + 3], mixing, liquid_first, i * quad, False, count))
            for i in range(2)
        ]

    def middle(arrived, flows):
        return [column_product(arrived[i], flows, illiquid_first, i * quad) for i in range(2)]

    def second_half(head, tail):
        quads = with_sides(head, tail)
        return [
            exchanged(mixed_product(*quads[i : i + 3], mixing, illiquid_second, i * quad, True, count))
            for i in range(2)
        ]

    def flow_columns(age):
        return exchanged(
            [lax.dynamic_slice_in_dim(utility[age], block * columns, columns, axis=2) for block in ahead]
        )

    coming = [shifted(values[0, i * quad : (i + 1) * quad], "age", -1) for i in range(2)]

    flows = flow_columns(0)
    arrived = first_half(values[1, :quad], values[1, quad:])
    arrived = second_half(*middle(arrived, flows))
    passed = [shifted(row_product(arrived[i], liquid_second, i * quad), "age", -1) for i in range(2)]

    flows = flow_columns(1)
    arrived = first_half(*coming)
    arrived = second_half(*middle(arrived, flows))

    whole = None
    for i in range(2):
        whole = last_sum(passed[i], i * quad, utility, 1, whole)
    for i in range(2):
        whole = last_rows(arrived[i], liquid_second, i * quad, utility, 0, whole)
    return whole


def solution(mesh):
    return jax.shard_map(
        local,
        mesh=mesh,
        in_specs=(
            P("age", "earn", "asset", None),
            P("age", "earn", "asset", None),
            P(None, "earn"),
            P("earn"),
            P("earn", None),
            P(None, "earn", None),
            P("earn", None),
            P(None, "earn", None),
        ),
        out_specs=P("age", "earn", "asset", None),
        check_vma=False,
    )
```

time: 696 us -> 365 us (0.52)
  waiting for transfers between devices: 318 us -> 153 us
  matrix products: 164 us -> 0 us
  Pallas kernels: 0 us -> 136 us
  local copies, waits for them, and re-layouts: 128 us -> 30.6 us
  other arithmetic: 41.4 us -> 0.22 us
    dot_general x6 -> x0, matrix products: 164 us -> none  [the longest x1 44.6 us: local(): jnp.einsum('ebc,texc->texb', illiquid_map, expected, precision=PRECISE)]
    pallas_call x0 -> x21, Pallas kernels: none -> 136 us  [the longest x8 69.1 us: mixed_product(): pl.pallas_call(functools.partial(mix_kernel, base, left_product, pieces),...]
    all_to_all x3 -> x0, waiting for transfers between devices: 85.8 us -> none  [the longest x1 45.4 us: to_rows(): lax.all_to_all(stacked, 'asset', split_axis=3, concat_axis=2, tiled=True)]
    all_to_all x6 -> x0, local copies, waits for them, and re-layouts: 80.6 us -> none  [the longest x4 53.8 us: to_columns(): lax.all_to_all(stacked, 'asset', split_axis=3, concat_axis=2, tiled=True)]
    ppermute x6 -> x22, waiting for transfers between devices: 233 us -> 153 us  [the longest x12 88.6 us: shifted(): lax.ppermute(value, axis, [(i, i + by) for i in range(count) if 0 <= i +...]
    transpose x2 -> x0, local copies, waits for them, and re-layouts: 26.4 us -> none  [the longest x1 13.2 us: local(): jnp.einsum('eac,tebc->teba', liquid_map, expected, precision=PRECISE)]
    ppermute x6 -> x22, starting transfers between devices: 16.3 us -> 41.7 us  [the longest x12 32.9 us: shifted(): lax.ppermute(value, axis, [(i, i + by) for i in range(count) if 0 <= i +...]
    dot_general x4 -> x0, other arithmetic: 25.3 us -> none  [the longest x1 7.15 us: local(): jnp.einsum('ebc,texc->texb', illiquid_map, expected, precision=PRECISE)]
  transfers between devices with their start and end apart: 9 -> 22, of which waited for: 8 -> 9; matrix products, arithmetic and copies ran while one was open for 19% -> 4% of each run, Pallas kernels for 0% -> 36%
where the time goes in v1:
time: 365 us; the launch traced here: 362 us
  waiting for transfers between devices  153 us (42%)
  Pallas kernels  136 us (37%)
  starting transfers between devices  41.7 us (11%)
  local copies, waits for them, and re-layouts  30.6 us (8%)
    ppermute x12, waiting for transfers between devices, shifted(): lax.ppermute(value, axis, [(i, i + by) for i in range(count) if 0 <= i +...  88.6 us
    pallas_call x8, Pallas kernels, mixed_product(): pl.pallas_call(functools.partial(mix_kernel, base, left_product, pieces),...  69.1 us
    ppermute x10, waiting for transfers between devices, exchanged(): lax.ppermute(pieces[s], 'asset', [(i, (i + s) % count) for i in range(cou...  64.8 us
    ppermute x12, starting transfers between devices, shifted(): lax.ppermute(value, axis, [(i, i + by) for i in range(count) if 0 <= i +...  32.9 us
    pallas_call x4, Pallas kernels, column_product(): pl.pallas_call(functools.partial(column_kernel, pieces), grid=(quad,), ou...  20.6 us
    pallas_call x3, Pallas kernels, band_pair(): pl.pallas_call(functools.partial(band_kernel, flip), grid=(states,), out_...  18.3 us
    pallas_call x2, Pallas kernels, last_rows(): pl.pallas_call(functools.partial(last_row_kernel, pieces), grid=(quad,),...  11.3 us
    unnamed x32, local copies, waits for them, and re-layouts  9.65 us
  transfers between devices with their start and end apart: 22, of which 9 were waited for; matrix products, arithmetic and copies ran while one was open for 4% of the time, Pallas kernels for 36%

profile of v1, /device:TPU:17, one launch (start us, length us, event | category | flops | bytes accessed | tf_op | source)
XLA Modules:
  0.0 362.2 jit_solution(15674407183040816108)
XLA Ops:
  0.0 6.9 %slice_bitcast_fusion = (f32[4,256,512]{2,1,0:T(8,128)S(1)}, f32[4,256,512]{2,1,0:T(8,128)}, f32[4,256,512]{2,1,0:T(8,128)}, f32[4,256,512]{2,1,0:T(8,128)}) fusion(f32[2,8,256,512]{3,2,1,0:T(8,128)} %param.8), kind=kLoop, calls=%fused_computation.2 | loop fusion | bytes 16777216 | tf_op jit(solution)/shard_map/squeeze | solution.py:377
  21.8 4.8 %dynamic-slice_bitcast_fusion = (f32[8,256,256]{2,1,0:T(8,128)}, f32[8,256,256]{2,1,0:T(8,128)}) fusion(f32[1,8,256,512]{3,2,1,0:T(8,128)} %get-tuple-element.49, s32[]{:T(128)S(6)} %select_n.59, s32[]{:T(128)S(6)} %select_n.61), kind=kLoop, calls=%fused_computation | loop fusion | bytes 8388616 | tf_op jit(solution)/shard_map/dynamic_slice | solution.py:371
  28.0 6.1 %band.5 = (bf16[8,512,512]{2,1,0:T(8,128)(2,1)S(1)}, bf16[8,512,512]{2,1,0:T(8,128)(2,1)}) custom-call(s32[2]{0:T(128)S(1)} %iota_multiply_fusion.bases, s32[8,1,512]{2,1,0:T(1,128)S(1)} %broadcast_in_dim.90.offset, f32[4,8,1,512]{3,2,1,0:T(1,128)S(1)} %broadcast_in_dim.91.weight), custom_call_target="tpu_custom_call" | custom-call | flops 25165824 | bytes 8388608 | tf_op jit(solution)/shard_map/band/pallas_call | solution.py:55
  39.6 7.7 %mix_band.13 = (f32[4,256,256]{2,1,0:T(8,128)S(1)}, f32[4,256,256]{2,1,0:T(8,128)S(1)}) custom-call(f32[8,9]{1,0:T(8,128)S(1)} %select_add_fusion.mixing, f32[4,256,512]{2,1,0:T(8,128)S(1)} %get-tuple-element.51.here.below, f32[4,256,512]{2,1,0:T(8,128)} %get-tuple-element.54.above.here, f32[4,256,512]{2,1,0:T(8,128)} %collective-permute-done.14.above, ...), custom_call_target="tpu_custom_call" | custom-call | flops 1610612736 | bytes 12582912 | tf_op jit(solution)/shard_map/mix_band/pallas_call | solution.py:130
  48.6 8.2 %mix_band.12 = (f32[4,256,256]{2,1,0:T(8,128)S(1)}, f32[4,256,256]{2,1,0:T(8,128)S(1)}) custom-call(f32[8,9]{1,0:T(8,128)S(1)} %select_add_fusion.mixing, f32[4,256,512]{2,1,0:T(8,128)} %collective-permute-done.11.below, f32[4,256,512]{2,1,0:T(8,128)} %copy-done.3, f32[4,256,512]{2,1,0:T(8,128)} %get-tuple-element.54.above.here, ...), custom_call_target="tpu_custom_call" | custom-call | flops 1610612736 | bytes 12582912 | tf_op jit(solution)/shard_map/mix_band/pallas_call | solution.py:130
  60.4 40.3 %collective-permute-done.above.here = f32[4,256,512]{2,1,0:T(8,128)} collective-permute-done((f32[4,256,512]{2,1,0:T(8,128)}, f32[4,256,512]{2,1,0:T(8,128)}, u32[]{:S(2)}, u32[]{:S(2)}) %collective-permute-start) | collective-permute-done | bytes 2097184 | tf_op jit(solution)/shard_map/ppermute | solution.py:283
  105.4 6.1 %band.4 = (bf16[8,512,512]{2,1,0:T(8,128)(2,1)S(1)}, bf16[8,512,512]{2,1,0:T(8,128)(2,1)}) custom-call(s32[2]{0:T(128)S(1)} %pad_add_fusion.2.bases, s32[8,1,512]{2,1,0:T(1,128)S(1)} %broadcast_in_dim.88.offset, f32[4,8,1,512]{3,2,1,0:T(1,128)S(1)} %broadcast_in_dim.89.weight), custom_call_target="tpu_custom_call" | custom-call | flops 25165824 | bytes 8388608 | tf_op jit(solution)/shard_map/band/pallas_call | solution.py:55
  120.1 5.7 %columns_band.6.below.here = f32[4,512,256]{2,1,0:T(8,128)} custom-call(bf16[8,512,512]{2,1,0:T(8,128)(2,1)} %copy-done, bf16[8,512,512]{2,1,0:T(8,128)(2,1)} %get-tuple-element.30.low, f32[4,256,256]{2,1,0:T(8,128)S(1)} %get-tuple-element.41.rest_0_, f32[4,256,256]{2,1,0:T(8,128)S(1)} %collective-permute-done.12.rest_1_, ...), custom_call_target="tpu_custom_call" | custom-call | flops 1610612736 | bytes 10485760 | tf_op jit(solution)/shard_map/columns_band/pallas_call | solution.py:173
  135.6 9.1 %mix_band.9 = (f32[4,256,256]{2,1,0:T(8,128)S(1)}, f32[4,256,256]{2,1,0:T(8,128)}) custom-call(f32[8,9]{1,0:T(8,128)S(1)} %select_add_fusion.mixing, f32[4,256,512]{2,1,0:T(8,128)} %collective-permute-done.2.here.below, f32[4,256,512]{2,1,0:T(8,128)} %collective-permute-done.above.here, f32[4,256,512]{2,1,0:T(8,128)} %copy-done.9, ...), custom_call_target="tpu_custom_call" | custom-call | flops 1610612736 | bytes 12582912 | tf_op jit(solution)/shard_map/mix_band/pallas_call | solution.py:130
  145.0 8.5 %mix_band.8 = (f32[4,256,256]{2,1,0:T(8,128)S(1)}, f32[4,256,256]{2,1,0:T(8,128)}) custom-call(f32[8,9]{1,0:T(8,128)S(1)} %select_add_fusion.mixing, f32[4,256,512]{2,1,0:T(8,128)S(1)} %collective-permute-done.1.below, f32[4,256,512]{2,1,0:T(8,128)} %collective-permute-done.2.here.below, f32[4,256,512]{2,1,0:T(8,128)} %collective-permute-done.above.here, ...), custom_call_target="tpu_custom_call" | custom-call | flops 1610612736 | bytes 12582912 | tf_op jit(solution)/shard_map/mix_band/pallas_call | solution.py:130
  154.8 9.0 %mix_band.15 = (f32[4,256,256]{2,1,0:T(8,128)S(1)}, f32[4,256,256]{2,1,0:T(8,128)}) custom-call(f32[8,9]{1,0:T(8,128)S(1)} %select_add_fusion.mixing, f32[4,512,256]{2,1,0:T(8,128)S(1)} %collective-permute-done.19.below, f32[4,512,256]{2,1,0:T(8,128)} %columns_band.6.below.here, f32[4,512,256]{2,1,0:T(8,128)} %copy-done.4, bf16[8,512,512]{2,1,0:T(8,128)(2,1)} %copy-done, ...), custom_call_target="tpu_custom_call" | custom-call | flops 1610612736 | bytes 12582912 | tf_op jit(solution)/shard_map/mix_band/pallas_call | solution.py:130
  164.1 9.6 %mix_band.14 = (f32[4,256,256]{2,1,0:T(8,128)S(1)}, f32[4,256,256]{2,1,0:T(8,128)}) custom-call(f32[8,9]{1,0:T(8,128)S(1)} %select_add_fusion.mixing, f32[4,512,256]{2,1,0:T(8,128)} %columns_band.6.below.here, f32[4,512,256]{2,1,0:T(8,128)} %copy-done.4, f32[4,512,256]{2,1,0:T(8,128)} %collective-permute-done.16.above, bf16[8,512,512]{2,1,0:T(8,128)(2,1)} %copy-done, ...), custom_call_target="tpu_custom_call" | custom-call | flops 1610612736 | bytes 12582912 | tf_op jit(solution)/shard_map/mix_band/pallas_call | solution.py:130
  175.0 5.9 %collective-permute-done.4.rest_3_ = f32[8,256,256]{2,1,0:T(8,128)} collective-permute-done((f32[8,256,256]{2,1,0:T(8,128)}, f32[8,256,256]{2,1,0:T(8,128)}, u32[]{:S(2)}, u32[]{:S(2)}) %collective-permute-start.4) | collective-permute-done | bytes 2097184 | tf_op jit(solution)/shard_map/ppermute | solution.py:289
  180.9 22.5 %collective-permute-done.6.rest_1_ = f32[4,256,256]{2,1,0:T(8,128)S(1)} collective-permute-done((f32[4,256,256]{2,1,0:T(8,128)}, f32[4,256,256]{2,1,0:T(8,128)S(1)}, u32[]{:S(2)}, u32[]{:S(2)}) %collective-permute-start.6) | collective-permute-done | bytes 1048608 | tf_op jit(solution)/shard_map/ppermute | solution.py:289
  211.9 14.0 %collective-permute-done.3.rest_1_ = f32[4,256,256]{2,1,0:T(8,128)S(1)} collective-permute-done((f32[4,256,256]{2,1,0:T(8,128)}, f32[4,256,256]{2,1,0:T(8,128)S(1)}, u32[]{:S(2)}, u32[]{:S(2)}) %collective-permute-start.3) | collective-permute-done | bytes 1048608 | tf_op jit(solution)/shard_map/ppermute | solution.py:289
  225.8 5.6 %columns_band.4.below.here = f32[4,512,256]{2,1,0:T(8,128)} custom-call(bf16[8,512,512]{2,1,0:T(8,128)(2,1)} %copy-done, bf16[8,512,512]{2,1,0:T(8,128)(2,1)} %get-tuple-element.30.low, f32[4,256,256]{2,1,0:T(8,128)S(1)} %get-tuple-element.33.rest_0_, f32[4,256,256]{2,1,0:T(8,128)S(1)} %collective-permute-done.3.rest_1_, ...), custom_call_target="tpu_custom_call" | custom-call | flops 1610612736 | bytes 10485760 | tf_op jit(solution)/shard_map/columns_band/pallas_call | solution.py:173
  233.7 6.1 %band.3 = (bf16[8,512,512]{2,1,0:T(8,128)(2,1)S(1)}, bf16[8,512,512]{2,1,0:T(8,128)(2,1)}) custom-call(s32[2]{0:T(128)S(1)} %pad_add_fusion.2.bases, s32[8,1,512]{2,1,0:T(1,128)S(1)} %broadcast_in_dim.75.offset, f32[4,8,1,512]{3,2,1,0:T(1,128)S(1)} %broadcast_in_dim.76.weight), custom_call_target="tpu_custom_call" | custom-call | flops 25165824 | bytes 8388608 | tf_op jit(solution)/shard_map/band/pallas_call | solution.py:55
  241.9 6.4 %collective-permute-done.20.rest_1_ = f32[4,256,256]{2,1,0:T(8,128)S(1)} collective-permute-done((f32[4,256,256]{2,1,0:T(8,128)}, f32[4,256,256]{2,1,0:T(8,128)S(1)}, u32[]{:S(2)}, u32[]{:S(2)}) %collective-permute-start.20) | collective-permute-done | bytes 1048608 | tf_op jit(solution)/shard_map/ppermute | solution.py:289
  254.6 16.0 %collective-permute-done.17.rest_1_ = f32[4,256,256]{2,1,0:T(8,128)S(1)} collective-permute-done((f32[4,256,256]{2,1,0:T(8,128)}, f32[4,256,256]{2,1,0:T(8,128)S(1)}, u32[]{:S(2)}, u32[]{:S(2)}) %collective-permute-start.17) | collective-permute-done | bytes 1048608 | tf_op jit(solution)/shard_map/ppermute | solution.py:289
  279.1 8.3 %mix_band.11 = (f32[4,256,256]{2,1,0:T(8,128)S(1)}, f32[4,256,256]{2,1,0:T(8,128)S(1)}) custom-call(f32[8,9]{1,0:T(8,128)S(1)} %select_add_fusion.mixing, f32[4,512,256]{2,1,0:T(8,128)S(1)} %collective-permute-done.9.below, f32[4,512,256]{2,1,0:T(8,128)} %columns_band.4.below.here, f32[4,512,256]{2,1,0:T(8,128)} %copy-done.5, bf16[8,512,512]{2,1,0:T(8,128)(2,1)} %copy-done, ...), custom_call_target="tpu_custom_call" | custom-call | flops 1610612736 | bytes 12582912 | tf_op jit(solution)/shard_map/mix_band/pallas_call | solution.py:130
  288.7 8.8 %mix_band.10 = (f32[4,256,256]{2,1,0:T(8,128)S(1)}, f32[4,256,256]{2,1,0:T(8,128)S(1)}) custom-call(f32[8,9]{1,0:T(8,128)S(1)} %select_add_fusion.mixing, f32[4,512,256]{2,1,0:T(8,128)} %columns_band.4.below.here, f32[4,512,256]{2,1,0:T(8,128)} %copy-done.5, f32[4,512,256]{2,1,0:T(8,128)} %collective-permute-done.7.above, bf16[8,512,512]{2,1,0:T(8,128)(2,1)} %copy-done, ...), custom_call_target="tpu_custom_call" | custom-call | flops 1610612736 | bytes 12582912 | tf_op jit(solution)/shard_map/mix_band/pallas_call | solution.py:130
  305.5 41.2 %collective-permute-done.18.arrived = f32[4,256,512]{2,1,0:T(8,128)} collective-permute-done((f32[4,256,512]{2,1,0:T(8,128)S(1)}, f32[4,256,512]{2,1,0:T(8,128)}, u32[]{:S(2)}, u32[]{:S(2)}) %collective-permute-start.18) | collective-permute-done | bytes 2097184 | tf_op jit(solution)/shard_map/ppermute | solution.py:283
  350.9 5.7 %last_rows.2.rest_2_ = f32[2,8,256,512]{3,2,1,0:T(8,128)} custom-call(bf16[8,512,512]{2,1,0:T(8,128)(2,1)} %copy-done.1, bf16[8,512,512]{2,1,0:T(8,128)(2,1)} %get-tuple-element.28.low, f32[2,8,256,512]{3,2,1,0:T(8,128)} %flow.7, f32[4,256,256]{2,1,0:T(8,128)S(1)} %get-tuple-element.39.rest_0_, ...), custom_call_target="tpu_custom_call", output_to_operand_aliasing={{}: (5, {})} | custom-call | flops 1610612736 | bytes 10485760 | tf_op jit(solution)/shard_map/last_rows/pallas_call | solution.py:240
  356.5 5.6 %last_rows.3 = f32[2,8,256,512]{3,2,1,0:T(8,128)} custom-call(bf16[8,512,512]{2,1,0:T(8,128)(2,1)} %copy-done.1, bf16[8,512,512]{2,1,0:T(8,128)(2,1)} %get-tuple-element.28.low, f32[2,8,256,512]{3,2,1,0:T(8,128)} %flow.7, f32[4,256,256]{2,1,0:T(8,128)S(1)} %get-tuple-element.37.rest_0_, ...), custom_call_target="tpu_custom_call", output_to_operand_aliasing={{}: (5, {})} | custom-call | flops 1610612736 | bytes 10485760 | tf_op jit(solution)/shard_map/last_rows/pallas_call | solution.py:240
  (96 shorter events, 93.6 us)
Async XLA Ops:
  6.9 32.6 %copy-start.3 = (f32[4,256,512]{2,1,0:T(8,128)}, f32[4,256,512]{2,1,0:T(8,128)S(1)}, u32[]{:S(2)}) copy-start(f32[4,256,512]{2,1,0:T(8,128)S(1)} %get-tuple-element.51.here.below) | copy-start | bytes 6291460
  6.9 50.2 %collective-permute-start.2 = (f32[4,256,512]{2,1,0:T(8,128)}, f32[4,256,512]{2,1,0:T(8,128)}, u32[]{:S(2)}, u32[]{:S(2)}) collective-permute-start(f32[4,256,512]{2,1,0:T(8,128)} %get-tuple-element.52), channel_id=1, source_target_pairs={{1,0},{2,1},{3,2},{5,4},{6,5},{7,6},{9,8},{10,9},{11,10},{13,12},{... | collective-permute-start | bytes 6291464 | tf_op jit(solution)/shard_map/ppermute | solution.py:283
  9.1 91.6 %collective-permute-start = (f32[4,256,512]{2,1,0:T(8,128)}, f32[4,256,512]{2,1,0:T(8,128)}, u32[]{:S(2)}, u32[]{:S(2)}) collective-permute-start(f32[4,256,512]{2,1,0:T(8,128)} %get-tuple-element.53), channel_id=1, source_target_pairs={{1,0},{2,1},{3,2},{5,4},{6,5},{7,6},{9,8},{10,9},{11,10},{13,12},{... | collective-permute-start | bytes 6291464 | tf_op jit(solution)/shard_map/ppermute | solution.py:283
  11.1 28.5 %collective-permute-start.14 = (f32[4,256,512]{2,1,0:T(8,128)S(1)}, f32[4,256,512]{2,1,0:T(8,128)}, u32[]{:S(2)}, u32[]{:S(2)}) collective-permute-start(f32[4,256,512]{2,1,0:T(8,128)S(1)} %get-tuple-element.51.here.below), channel_id=1, source_target_pairs={{4,0},{8,4},{12,8},{5,1},{9,5},{13,9},{6,2},{10,6},{14,10},{7,3},{... | collective-permute-start | bytes 6291464 | tf_op jit(solution)/shard_map/ppermute | solution.py:283
  13.9 34.6 %collective-permute-start.11 = (f32[4,256,512]{2,1,0:T(8,128)}, f32[4,256,512]{2,1,0:T(8,128)}, u32[]{:S(2)}, u32[]{:S(2)}) collective-permute-start(f32[4,256,512]{2,1,0:T(8,128)} %get-tuple-element.54.above.here), channel_id=1, source_target_pairs={{0,4},{4,8},{8,12},{1,5},{5,9},{9,13},{2,6},{6,10},{10,14},{3,7},{... | collective-permute-start | bytes 6291464 | tf_op jit(solution)/shard_map/ppermute | solution.py:283
  26.6 87.0 %collective-permute-start.13 = (f32[8,256,256]{2,1,0:T(8,128)}, f32[8,256,256]{2,1,0:T(8,128)}, u32[]{:S(2)}, u32[]{:S(2)}) collective-permute-start(f32[8,256,256]{2,1,0:T(8,128)} %get-tuple-element.55), channel_id=1, source_target_pairs={{0,16},{16,0},{1,17},{17,1},{2,18},{18,2},{3,19},{19,3},{4,20},{20... | collective-permute-start | bytes 6291464 | tf_op jit(solution)/shard_map/ppermute | solution.py:289
  47.3 66.3 %collective-permute-start.15 = (f32[4,256,256]{2,1,0:T(8,128)S(1)}, f32[4,256,256]{2,1,0:T(8,128)S(1)}, u32[]{:S(2)}, u32[]{:S(2)}) collective-permute-start(f32[4,256,256]{2,1,0:T(8,128)S(1)} %get-tuple-element.44), channel_id=1, source_target_pairs={{0,16},{16,0},{1,17},{17,1},{2,18},{18,2},{3,19},{19,3},{4,20},{20... | collective-permute-start | bytes 3145736 | tf_op jit(solution)/shard_map/ppermute | solution.py:289
  56.8 63.3 %collective-permute-start.12 = (f32[4,256,256]{2,1,0:T(8,128)S(1)}, f32[4,256,256]{2,1,0:T(8,128)S(1)}, u32[]{:S(2)}, u32[]{:S(2)}) collective-permute-start(f32[4,256,256]{2,1,0:T(8,128)S(1)} %get-tuple-element.42), channel_id=1, source_target_pairs={{0,16},{16,0},{1,17},{17,1},{2,18},{18,2},{3,19},{19,3},{4,20},{20... | collective-permute-start | bytes 3145736 | tf_op jit(solution)/shard_map/ppermute | solution.py:289
  57.1 77.2 %collective-permute-start.5 = (f32[4,256,512]{2,1,0:T(8,128)}, f32[4,256,512]{2,1,0:T(8,128)S(1)}, u32[]{:S(2)}, u32[]{:S(2)}) collective-permute-start(f32[4,256,512]{2,1,0:T(8,128)} %collective-permute-done.2.here.below), channel_id=1, source_target_pairs={{4,0},{8,4},{12,8},{5,1},{9,5},{13,9},{6,2},{10,6},{14,10},{7,3},{... | collective-permute-start | bytes 6291464 | tf_op jit(solution)/shard_map/ppermute | solution.py:283
  100.7 44.3 %collective-permute-start.1 = (f32[4,256,512]{2,1,0:T(8,128)}, f32[4,256,512]{2,1,0:T(8,128)S(1)}, u32[]{:S(2)}, u32[]{:S(2)}) collective-permute-start(f32[4,256,512]{2,1,0:T(8,128)} %collective-permute-done.above.here), channel_id=1, source_target_pairs={{0,4},{4,8},{8,12},{1,5},{5,9},{9,13},{2,6},{6,10},{10,14},{3,7},{... | collective-permute-start | bytes 6291464 | tf_op jit(solution)/shard_map/ppermute | solution.py:283
  118.2 36.6 %collective-permute-start.19 = (f32[4,512,256]{2,1,0:T(8,128)S(1)}, f32[4,512,256]{2,1,0:T(8,128)S(1)}, u32[]{:S(2)}, u32[]{:S(2)}) collective-permute-start(f32[4,512,256]{2,1,0:T(8,128)S(1)} %columns_band.7.here.above), channel_id=1, source_target_pairs={{0,4},{4,8},{8,12},{1,5},{5,9},{9,13},{2,6},{6,10},{10,14},{3,7},{... | collective-permute-start | bytes 6291464 | tf_op jit(solution)/shard_map/ppermute | solution.py:283
  125.8 38.2 %collective-permute-start.16 = (f32[4,512,256]{2,1,0:T(8,128)}, f32[4,512,256]{2,1,0:T(8,128)}, u32[]{:S(2)}, u32[]{:S(2)}) collective-permute-start(f32[4,512,256]{2,1,0:T(8,128)} %columns_band.6.below.here), channel_id=1, source_target_pairs={{4,0},{8,4},{12,8},{5,1},{9,5},{13,9},{6,2},{10,6},{14,10},{7,3},{... | collective-permute-start | bytes 6291464 | tf_op jit(solution)/shard_map/ppermute | solution.py:283
  133.0 47.9 %collective-permute-start.4 = (f32[8,256,256]{2,1,0:T(8,128)}, f32[8,256,256]{2,1,0:T(8,128)}, u32[]{:S(2)}, u32[]{:S(2)}) collective-permute-start(f32[8,256,256]{2,1,0:T(8,128)} %get-tuple-element.57), channel_id=1, source_target_pairs={{0,16},{16,0},{1,17},{17,1},{2,18},{18,2},{3,19},{19,3},{4,20},{20... | collective-permute-start | bytes 6291464 | tf_op jit(solution)/shard_map/ppermute | solution.py:289
  144.7 58.7 %collective-permute-start.6 = (f32[4,256,256]{2,1,0:T(8,128)}, f32[4,256,256]{2,1,0:T(8,128)S(1)}, u32[]{:S(2)}, u32[]{:S(2)}) collective-permute-start(f32[4,256,256]{2,1,0:T(8,128)} %get-tuple-element.36), channel_id=1, source_target_pairs={{0,16},{16,0},{1,17},{17,1},{2,18},{18,2},{3,19},{19,3},{4,20},{20... | collective-permute-start | bytes 3145736 | tf_op jit(solution)/shard_map/ppermute | solution.py:289
  153.5 72.4 %collective-permute-start.3 = (f32[4,256,256]{2,1,0:T(8,128)}, f32[4,256,256]{2,1,0:T(8,128)S(1)}, u32[]{:S(2)}, u32[]{:S(2)}) collective-permute-start(f32[4,256,256]{2,1,0:T(8,128)} %get-tuple-element.34), channel_id=1, source_target_pairs={{0,16},{16,0},{1,17},{17,1},{2,18},{18,2},{3,19},{19,3},{4,20},{20... | collective-permute-start | bytes 3145736 | tf_op jit(solution)/shard_map/ppermute | solution.py:289
  163.8 84.5 %collective-permute-start.20 = (f32[4,256,256]{2,1,0:T(8,128)}, f32[4,256,256]{2,1,0:T(8,128)S(1)}, u32[]{:S(2)}, u32[]{:S(2)}) collective-permute-start(f32[4,256,256]{2,1,0:T(8,128)} %get-tuple-element.48), channel_id=1, source_target_pairs={{0,16},{16,0},{1,17},{17,1},{2,18},{18,2},{3,19},{19,3},{4,20},{20... | collective-permute-start | bytes 3145736 | tf_op jit(solution)/shard_map/ppermute | solution.py:289
  173.7 96.9 %collective-permute-start.17 = (f32[4,256,256]{2,1,0:T(8,128)}, f32[4,256,256]{2,1,0:T(8,128)S(1)}, u32[]{:S(2)}, u32[]{:S(2)}) collective-permute-start(f32[4,256,256]{2,1,0:T(8,128)} %get-tuple-element.46), channel_id=1, source_target_pairs={{0,16},{16,0},{1,17},{17,1},{2,18},{18,2},{3,19},{19,3},{4,20},{20... | collective-permute-start | bytes 3145736 | tf_op jit(solution)/shard_map/ppermute | solution.py:289
  208.0 23.5 %copy-start.5 = (f32[4,512,256]{2,1,0:T(8,128)}, f32[4,512,256]{2,1,0:T(8,128)S(1)}, u32[]{:S(2)}) copy-start(f32[4,512,256]{2,1,0:T(8,128)S(1)} %columns_band.5.here.above) | copy-start | bytes 6291460
  208.0 71.1 %collective-permute-start.9 = (f32[4,512,256]{2,1,0:T(8,128)S(1)}, f32[4,512,256]{2,1,0:T(8,128)S(1)}, u32[]{:S(2)}, u32[]{:S(2)}) collective-permute-start(f32[4,512,256]{2,1,0:T(8,128)S(1)} %columns_band.5.here.above), channel_id=1, source_target_pairs={{0,4},{4,8},{8,12},{1,5},{5,9},{9,13},{2,6},{6,10},{10,14},{3,7},{... | collective-permute-start | bytes 6291464 | tf_op jit(solution)/shard_map/ppermute | solution.py:283
  231.5 57.2 %collective-permute-start.7 = (f32[4,512,256]{2,1,0:T(8,128)}, f32[4,512,256]{2,1,0:T(8,128)}, u32[]{:S(2)}, u32[]{:S(2)}) collective-permute-start(f32[4,512,256]{2,1,0:T(8,128)} %columns_band.4.below.here), channel_id=1, source_target_pairs={{4,0},{8,4},{12,8},{5,1},{9,5},{13,9},{6,2},{10,6},{14,10},{7,3},{... | collective-permute-start | bytes 6291464 | tf_op jit(solution)/shard_map/ppermute | solution.py:283
  252.5 49.1 %collective-permute-start.21 = (f32[4,256,512]{2,1,0:T(8,128)S(1)}, f32[4,256,512]{2,1,0:T(8,128)S(1)}, u32[]{:S(2)}, u32[]{:S(2)}) collective-permute-start(f32[4,256,512]{2,1,0:T(8,128)S(1)} %rows_band.3), channel_id=1, source_target_pairs={{1,0},{2,1},{3,2},{5,4},{6,5},{7,6},{9,8},{10,9},{11,10},{13,12},{... | collective-permute-start | bytes 6291464 | tf_op jit(solution)/shard_map/ppermute | solution.py:283
  277.0 69.6 %collective-permute-start.18 = (f32[4,256,512]{2,1,0:T(8,128)S(1)}, f32[4,256,512]{2,1,0:T(8,128)}, u32[]{:S(2)}, u32[]{:S(2)}) collective-permute-start(f32[4,256,512]{2,1,0:T(8,128)S(1)} %rows_band.2), channel_id=1, source_target_pairs={{1,0},{2,1},{3,2},{5,4},{6,5},{7,6},{9,8},{10,9},{11,10},{13,12},{... | collective-permute-start | bytes 6291464 | tf_op jit(solution)/shard_map/ppermute | solution.py:283
  287.4 63.5 %collective-permute-start.10 = (f32[4,256,256]{2,1,0:T(8,128)S(1)}, f32[4,256,256]{2,1,0:T(8,128)S(1)}, u32[]{:S(2)}, u32[]{:S(2)}) collective-permute-start(f32[4,256,256]{2,1,0:T(8,128)S(1)} %get-tuple-element.40), channel_id=1, source_target_pairs={{0,16},{16,0},{1,17},{17,1},{2,18},{18,2},{3,19},{19,3},{4,20},{20... | collective-permute-start | bytes 3145736 | tf_op jit(solution)/shard_map/ppermute | solution.py:289
  297.5 59.0 %collective-permute-start.8 = (f32[4,256,256]{2,1,0:T(8,128)S(1)}, f32[4,256,256]{2,1,0:T(8,128)S(1)}, u32[]{:S(2)}, u32[]{:S(2)}) collective-permute-start(f32[4,256,256]{2,1,0:T(8,128)S(1)} %get-tuple-element.38), channel_id=1, source_target_pairs={{0,16},{16,0},{1,17},{17,1},{2,18},{18,2},{3,19},{19,3},{4,20},{20... | collective-permute-start | bytes 3145736 | tf_op jit(solution)/shard_map/ppermute | solution.py:289
  (14 other events, 87.7 us)

commit v2 on v1

--- a/solution.py
+++ b/solution.py
@@ -11,11 +11,26 @@
 BAND = 4
 DISCOUNT = 0.96
 SPAN = 2 * REACH + 1
-VMEM_BYTES = 48 * 1024 * 1024
+VMEM_BYTES = 60 * 1024 * 1024
 
 
 def params():
     return pltpu.CompilerParams(vmem_limit_bytes=VMEM_BYTES)
+
+
+def ordered_call(kernel, after, in_specs, **rest):
+    known, extra = len(in_specs), len(after)
+
+    def body(*refs):
+        kernel(*refs[:known], *refs[known + extra :])
+
+    call = pl.pallas_call(
+        body,
+        in_specs=list(in_specs) + [pl.BlockSpec(memory_space=pl.ANY)] * extra,
+        compiler_params=params(),
+        **rest,
+    )
+    return lambda *operands: call(*operands, *after)
 
 
 def halves(x):
@@ -71,14 +86,15 @@
     )(bases, offset[:, None, :], weight[:, :, None, :])
 
 
-def mix_kernel(base, left_product, pieces, mixing, below, here, above, high, low, *rest):
+def mix_kernel(base, left_product, pieces, places, mixing, below, here, above, high, low, *rest):
     outs, (slabs, xh, xl, sems) = rest[:pieces], rest[pieces:]
     e = pl.program_id(0)
-    quad = here.shape[0]
+    quad = slabs.shape[0] // 3
 
     def fetch(source, group):
+        place = places[group]
         return [
-            pltpu.make_async_copy(source.at[i], slabs.at[group * quad + i], sems.at[group * quad + i])
+            pltpu.make_async_copy(source.at[i] if place is None else source.at[place[0], place[1] + i], slabs.at[group * quad + i], sems.at[group * quad + i])
             for i in range(quad)
         ]
 
@@ -122,13 +138,17 @@
             outs[s][0] = result[:, s * width : (s + 1) * width]
 
 
-def mixed_product(below, here, above, mixing, pair, base, left_product, pieces):
-    quad, rows, columns = here.shape
+def mixed_product(sources, mixing, pair, base, left_product, pieces, after=()):
+    quad = REACH
+    arrays = [source[0] if isinstance(source, tuple) else source for source in sources]
+    places = [source[1:] if isinstance(source, tuple) else None for source in sources]
+    rows, columns = arrays[0].shape[-2:]
     extent = pair[0].shape[1]
     shape = (rows // pieces, columns) if left_product else (rows, columns // pieces)
     matrix = pl.BlockSpec((1, extent, extent), lambda e: (base + e, 0, 0))
-    return pl.pallas_call(
-        functools.partial(mix_kernel, base, left_product, pieces),
+    return ordered_call(
+        functools.partial(mix_kernel, base, left_product, pieces, places),
+        after,
         grid=(quad,),
         out_shape=[jax.ShapeDtypeStruct((quad,) + shape, jnp.float32)] * pieces,
         in_specs=[pl.BlockSpec(memory_space=pltpu.SMEM)]
@@ -141,14 +161,13 @@
             pltpu.VMEM((rows, columns), jnp.bfloat16),
             pltpu.SemaphoreType.DMA((3 * quad,)),
         ],
-        compiler_params=params(),
         cost_estimate=pl.CostEstimate(
             flops=quad * rows * columns * extent * 6,
             bytes_accessed=4 * quad * rows * columns * 4 + 4 * quad * extent * extent,
             transcendentals=0,
         ),
         name="mix_band",
-    )(mixing, below, here, above, *pair)
+    )(mixing, *arrays, *pair)
 
 
 def column_kernel(pieces, high, low, *rest):
@@ -163,21 +182,20 @@
         out[0, at, :] = flows[s][0] + DISCOUNT * result[s * rows : (s + 1) * rows]
 
 
-def column_product(parts, flows, pair, base):
+def column_product(parts, flows, pair, base, after=()):
     pieces = len(parts)
     quad, rows, columns = parts[0].shape
     extent = pair[0].shape[1]
     matrix = pl.BlockSpec((1, extent, extent), lambda e: (base + e, 0, 0))
     piece = pl.BlockSpec((1, rows, columns), lambda e: (e, 0, 0))
-    flow = pl.BlockSpec((1, rows, columns), lambda e: (base + e, 0, 0))
-    return pl.pallas_call(
+    return ordered_call(
         functools.partial(column_kernel, pieces),
+        after,
         grid=(quad,),
         out_shape=jax.ShapeDtypeStruct((quad, extent, columns), jnp.float32),
-        in_specs=[matrix] * 2 + [piece] * pieces + [flow] * pieces,
+        in_specs=[matrix] * 2 + [piece] * (2 * pieces),
         out_specs=pl.BlockSpec((1, extent, columns), lambda e: (e, 0, 0)),
         scratch_shapes=[pltpu.VMEM((extent, columns), jnp.bfloat16)] * 2,
-        compiler_params=params(),
         cost_estimate=pl.CostEstimate(
             flops=quad * extent * columns * extent * 6,
             bytes_accessed=3 * quad * extent * columns * 4 + 4 * quad * extent * extent,
@@ -198,84 +216,61 @@
     return result
 
 
-def row_kernel(pieces, high, low, *rest):
-    parts, out = rest[:pieces], rest[pieces]
-    out[0] = row_product_of(parts, high, low)
-
-
-def row_product(parts, pair, base):
-    pieces = len(parts)
-    quad, rows, columns = parts[0].shape
-    extent = pair[0].shape[1]
-    matrix = pl.BlockSpec((1, extent, extent), lambda e: (base + e, 0, 0))
-    piece = pl.BlockSpec((1, rows, columns), lambda e: (e, 0, 0))
-    return pl.pallas_call(
-        functools.partial(row_kernel, pieces),
-        grid=(quad,),
-        out_shape=jax.ShapeDtypeStruct((quad, rows, extent), jnp.float32),
-        in_specs=[matrix] * 2 + [piece] * pieces,
-        out_specs=pl.BlockSpec((1, rows, extent), lambda e: (e, 0, 0)),
-        compiler_params=params(),
-        cost_estimate=pl.CostEstimate(
-            flops=quad * rows * extent * extent * 6,
-            bytes_accessed=2 * quad * rows * extent * 4 + 4 * quad * extent * extent,
-            transcendentals=0,
-        ),
-        name="rows_band",
-    )(*pair, *parts)
-
-
 def last_row_kernel(pieces, high, low, flow, *rest):
     parts, out = rest[:pieces], rest[-1]
     out[0, 0] = flow[0, 0] + DISCOUNT * row_product_of(parts, high, low)
 
 
-def last_rows(parts, pair, base, utility, age, whole):
+def last_rows(parts, pair, base, utility, age, whole, after=()):
     pieces = len(parts)
     quad, rows, columns = parts[0].shape
     extent = pair[0].shape[1]
     matrix = pl.BlockSpec((1, extent, extent), lambda e: (base + e, 0, 0))
     piece = pl.BlockSpec((1, rows, columns), lambda e: (e, 0, 0))
     flow = pl.BlockSpec((1, 1, rows, extent), lambda e: (age, base + e, 0, 0))
-    return pl.pallas_call(
+    before = () if whole is None else (whole,)
+    return ordered_call(
         functools.partial(last_row_kernel, pieces),
+        after,
         grid=(quad,),
         out_shape=jax.ShapeDtypeStruct(utility.shape, jnp.float32),
-        in_specs=[matrix] * 2 + [flow] + [piece] * pieces + [pl.BlockSpec(memory_space=pl.ANY)],
+        in_specs=[matrix] * 2 + [flow] + [piece] * pieces + [pl.BlockSpec(memory_space=pl.ANY)] * len(before),
         out_specs=flow,
-        input_output_aliases={3 + pieces: 0},
-        compiler_params=params(),
+        input_output_aliases={} if whole is None else {3 + pieces: 0},
         cost_estimate=pl.CostEstimate(
             flops=quad * rows * extent * extent * 6,
             bytes_accessed=3 * quad * rows * extent * 4 + 4 * quad * extent * extent,
             transcendentals=0,
         ),
         name="last_rows",
-    )(*pair, utility, *parts, whole)
-
-
-def add_kernel(flow, arrived, *rest):
-    rest[-1][0, 0] = flow[0, 0] + DISCOUNT * arrived[0]
-
-
-def last_sum(arrived, base, utility, age, whole):
-    quad, rows, extent = arrived.shape
-    flow = pl.BlockSpec((1, 1, rows, extent), lambda e: (age, base + e, 0, 0))
-    part = pl.BlockSpec((1, rows, extent), lambda e: (e, 0, 0))
-    before = () if whole is None else (whole,)
+    )(*pair, utility, *parts, *before)
+
+
+def take_kernel(place, flow, out):
+    out[0] = flow[0, 0]
+
+
+def taken_columns(utility, age, base, block, columns, after=()):
+    quad = REACH
+    rows = utility.shape[2]
+    if columns % 128:
+        return lax.dynamic_slice_in_dim(utility[age, base : base + quad], block * columns, columns, axis=2)
     return pl.pallas_call(
-        add_kernel,
-        grid=(quad,),
-        out_shape=jax.ShapeDtypeStruct(utility.shape, jnp.float32),
-        in_specs=[flow, part] + [pl.BlockSpec(memory_space=pl.ANY)] * len(before),
-        out_specs=flow,
-        input_output_aliases={} if whole is None else {2: 0},
+        lambda place, flow, *rest: take_kernel(place, flow, rest[-1]),
+        out_shape=jax.ShapeDtypeStruct((quad, rows, columns), jnp.float32),
+        grid_spec=pltpu.PrefetchScalarGridSpec(
+            num_scalar_prefetch=1,
+            grid=(quad,),
+            in_specs=[pl.BlockSpec((1, 1, rows, columns), lambda e, place: (age, base + e, 0, place[0]))]
+            + [pl.BlockSpec(memory_space=pl.ANY)] * len(after),
+            out_specs=pl.BlockSpec((1, rows, columns), lambda e, place: (e, 0, 0)),
+        ),
         compiler_params=params(),
         cost_estimate=pl.CostEstimate(
-            flops=quad * rows * extent * 2, bytes_accessed=3 * quad * rows * extent * 4, transcendentals=0
-        ),
-        name="last_sum",
-    )(utility, arrived, *before)
+            flops=0, bytes_accessed=2 * quad * rows * columns * 4, transcendentals=0
+        ),
+        name="take",
+    )(jnp.reshape(jnp.asarray(block, jnp.int32), (1,)), utility, *after)
 
 
 def shifted(value, axis, by):
@@ -283,11 +278,22 @@
     return lax.ppermute(value, axis, [(i, i + by) for i in range(count) if 0 <= i + by < count])
 
 
-def exchanged(pieces):
-    count = lax.axis_size("asset")
-    return [pieces[0]] + [
-        lax.ppermute(pieces[s], "asset", [(i, (i + s) % count) for i in range(count)])
-        for s in range(1, count)
+def exchanged(pieces, by=0):
+    count, ages = lax.axis_size("asset"), lax.axis_size("age")
+    return [
+        piece
+        if s == 0 and by == 0
+        else lax.ppermute(
+            piece,
+            ("asset", "age"),
+            [
+                (a * ages + z, (a + s) % count * ages + z + by)
+                for a in range(count)
+                for z in range(ages)
+                if 0 <= z + by < ages
+            ],
+        )
+        for s, piece in enumerate(pieces)
     ]
 
 
@@ -346,48 +352,54 @@
         slot = support_start + number - own + REACH
         mixing = mixing + jnp.where(slots[None, :] == slot[:, None], shares[number][:, None], 0.0)
 
-    def with_sides(head, tail):
-        return [shifted(tail, "earn", 1), head, tail, shifted(head, "earn", -1)]
-
-    def first_half(head, tail):
-        quads = with_sides(head, tail)
-        return [
-            exchanged(mixed_product(*quads[i : i + 3], mixing, liquid_first, i * quad, False, count))
-            for i in range(2)
-        ]
-
-    def middle(arrived, flows):
-        return [column_product(arrived[i], flows, illiquid_first, i * quad) for i in range(2)]
-
-    def second_half(head, tail):
-        quads = with_sides(head, tail)
-        return [
-            exchanged(mixed_product(*quads[i : i + 3], mixing, illiquid_second, i * quad, True, count))
-            for i in range(2)
-        ]
-
-    def flow_columns(age):
-        return exchanged(
-            [lax.dynamic_slice_in_dim(utility[age], block * columns, columns, axis=2) for block in ahead]
-        )
-
-    coming = [shifted(values[0, i * quad : (i + 1) * quad], "age", -1) for i in range(2)]
-
-    flows = flow_columns(0)
-    arrived = first_half(values[1, :quad], values[1, quad:])
-    arrived = second_half(*middle(arrived, flows))
-    passed = [shifted(row_product(arrived[i], liquid_second, i * quad), "age", -1) for i in range(2)]
-
-    flows = flow_columns(1)
-    arrived = first_half(*coming)
-    arrived = second_half(*middle(arrived, flows))
-
-    whole = None
-    for i in range(2):
-        whole = last_sum(passed[i], i * quad, utility, 1, whole)
-    for i in range(2):
-        whole = last_rows(arrived[i], liquid_second, i * quad, utility, 0, whole)
-    return whole
+    def first_half(age, by, after):
+        left = shifted(values[age, quad:], "earn", 1)
+        right = shifted(values[age, :quad], "earn", -1)
+        head, tail = (values, age, 0), (values, age, quad)
+        parts = [mixed_product((left, head, tail), mixing, liquid_first, 0, False, count, after)]
+        parts.append(mixed_product((head, tail, right), mixing, liquid_first, quad, False, count, (parts[0][0],)))
+        return parts[1][0], [exchanged(part, by) for part in parts]
+
+    def flow_columns(age, i, after):
+        parts = [taken_columns(utility, age, i * quad, block, columns, after) for block in ahead]
+        return parts[0], exchanged(parts)
+
+    def middle(arrived, flows, i, after):
+        return column_product(arrived[i], flows[i], illiquid_first, i * quad, after)
+
+    def second_half(sides, i, after):
+        return mixed_product(sides, mixing, illiquid_second, i * quad, True, count, after)
+
+    done, flow_a = zip(*[flow_columns(0, i, ()) for i in range(2)])
+    done, arrived_a = first_half(1, 0, tuple(done))
+    done, arrived_b = first_half(0, -1, (done,))
+
+    head_a = middle(arrived_a, flow_a, 0, (done,))
+    right_a = shifted(head_a, "earn", -1)
+    tail_a = middle(arrived_a, flow_a, 1, (head_a,))
+    left_a = shifted(tail_a, "earn", 1)
+    first, flow_b0 = flow_columns(1, 0, (tail_a,))
+    second, flow_b1 = flow_columns(1, 1, (first,))
+    flow_b = (flow_b0, flow_b1)
+
+    parts = second_half((head_a, tail_a, right_a), 1, (second,))
+    last_a1 = exchanged(parts, -1)
+    head_b = middle(arrived_b, flow_b, 0, (parts[0],))
+    right_b = shifted(head_b, "earn", -1)
+    parts = second_half((left_a, head_a, tail_a), 0, (head_b,))
+    last_a0 = exchanged(parts, -1)
+    tail_b = middle(arrived_b, flow_b, 1, (parts[0],))
+    left_b = shifted(tail_b, "earn", 1)
+
+    parts = second_half((head_b, tail_b, right_b), 1, (tail_b,))
+    last_b1 = exchanged(parts)
+    parts = second_half((left_b, head_b, tail_b), 0, (parts[0],))
+    last_b0 = exchanged(parts)
+
+    whole = last_rows(last_a1, liquid_second, quad, utility, 1, None, (parts[0],))
+    whole = last_rows(last_a0, liquid_second, 0, utility, 1, whole)
+    whole = last_rows(last_b1, liquid_second, quad, utility, 0, whole)
+    return last_rows(last_b0, liquid_second, 0, utility, 0, whole)
 
 
 def solution(mesh):

time: 365 us -> 359 us (0.984)
  Pallas kernels: 136 us -> 173 us
  waiting for transfers between devices: 153 us -> 122 us
  local copies, waits for them, and re-layouts: 30.6 us -> 13.1 us
    ppermute x12 -> x8, waiting for transfers between devices: 88.6 us -> 5.48 us  [shifted(): lax.ppermute(value, axis, [(i, i + by) for i in range(count) if 0 <= i +...]
    ppermute x10 -> x16, waiting for transfers between devices: 64.8 us -> 117 us  [exchanged(): lax.ppermute(piece, ('asset', 'age'), [(a * ages + z, (a + s) % count * a...]
    pallas_call x18 -> x24, Pallas kernels: 118 us -> 152 us  [the longest x16 125 us: ordered_call(): return lambda *operands: call(*operands, *after)]
    ppermute x10 -> x16, starting transfers between devices: 8.86 us -> 23.9 us  [exchanged(): lax.ppermute(piece, ('asset', 'age'), [(a * ages + z, (a + s) % count * a...]
    ppermute x12 -> x8, starting transfers between devices: 32.9 us -> 21.1 us  [shifted(): lax.ppermute(value, axis, [(i, i + by) for i in range(count) if 0 <= i +...]
    dynamic_slice x2 -> x0, local copies, waits for them, and re-layouts: 9.43 us -> none  [flow_columns(): lax.dynamic_slice_in_dim(utility[age], block * columns, columns, axis=2)]
    unnamed x32 -> x24, local copies, waits for them, and re-layouts: 9.65 us -> 2.72 us
    slice x1 -> x0, local copies, waits for them, and re-layouts: 4.36 us -> none  [flow_columns(): utility[age]]
  transfers between devices with their start and end apart: 22 -> 24, of which waited for: 9 -> 10; matrix products, arithmetic and copies ran while one was open for 4% -> 2% of each run, Pallas kernels for 36% -> 47%
where the time goes in v2:
time: 359 us; the launch traced here: 356 us
  Pallas kernels  173 us (48%)
  waiting for transfers between devices  122 us (34%)
  starting transfers between devices  45.1 us (13%)
  local copies, waits for them, and re-layouts  13.1 us (4%)
    pallas_call x16, Pallas kernels, ordered_call(): return lambda *operands: call(*operands, *after)  125 us
    ppermute x16, waiting for transfers between devices, exchanged(): lax.ppermute(piece, ('asset', 'age'), [(a * ages + z, (a + s) % count * a...  117 us
    pallas_call x8, Pallas kernels, taken_columns(): pl.pallas_call(lambda place, flow, *rest: take_kernel(place, flow, rest[-...  27.2 us
    ppermute x16, starting transfers between devices, exchanged(): lax.ppermute(piece, ('asset', 'age'), [(a * ages + z, (a + s) % count * a...  23.9 us
    pallas_call x3, Pallas kernels, band_pair(): pl.pallas_call(functools.partial(band_kernel, flip), grid=(states,), out_...  21.5 us
    ppermute x8, starting transfers between devices, shifted(): lax.ppermute(value, axis, [(i, i + by) for i in range(count) if 0 <= i +...  21.1 us
  transfers between devices with their start and end apart: 24, of which 10 were waited for; matrix products, arithmetic and copies ran while one was open for 2% of the time, Pallas kernels for 47%

profile of v2, /device:TPU:17, one launch (start us, length us, event | category | flops | bytes accessed | tf_op | source)
XLA Modules:
  0.0 355.9 jit_solution(5549707891215191371)
XLA Ops:
  0.0 6.6 %slice_bitcast_fusion = (f32[4,256,512]{2,1,0:T(8,128)}, f32[4,256,512]{2,1,0:T(8,128)}, f32[4,256,512]{2,1,0:T(8,128)}, f32[4,256,512]{2,1,0:T(8,128)S(1)}) fusion(f32[2,8,256,512]{3,2,1,0:T(8,128)} %refs_2_.11), kind=kLoop, calls=%fused_computation | loop fusion | bytes 16777216 | tf_op jit(solution)/shard_map/squeeze | solution.py:356
  31.3 7.1 %band.5 = (bf16[8,512,512]{2,1,0:T(8,128)(2,1)}, bf16[8,512,512]{2,1,0:T(8,128)(2,1)}) custom-call(s32[2]{0:T(128)} %iota_multiply_fusion.bases, s32[8,1,512]{2,1,0:T(1,128)} %broadcast_in_dim.90.offset, f32[4,8,1,512]{3,2,1,0:T(1,128)} %broadcast_in_dim.91.weight), custom_call_target="tpu_custom_call" | custom-call | flops 25165824 | bytes 8388608 | tf_op jit(solution)/shard_map/band/pallas_call | solution.py:70
  39.1 9.3 %mix_band.8 = (f32[4,256,256]{2,1,0:T(8,128)}, f32[4,256,256]{2,1,0:T(8,128)}) custom-call(f32[8,9]{1,0:T(8,128)} %select_add_fusion.refs_0_, f32[4,256,512]{2,1,0:T(8,128)} %collective-permute-done.3.refs_1_, f32[2,8,256,512]{3,2,1,0:T(8,128)} %refs_2_.11, f32[2,8,256,512]{3,2,1,0:T(8,128)} %refs_2_.11, bf16[8,512,512]{2,1,0:T(8,128)(2,1)} %get-tuple-element.31.refs_4_, ...), custom_call_target="tpu_custom_call" | custom-call | flops 1610612736 | bytes 12582912 | tf_op jit(solution)/shard_map/mix_band/pallas_call | solution.py:33
  54.0 7.3 %band.4 = (bf16[8,512,512]{2,1,0:T(8,128)(2,1)}, bf16[8,512,512]{2,1,0:T(8,128)(2,1)}) custom-call(s32[2]{0:T(128)} %pad_add_fusion.2.bases, s32[8,1,512]{2,1,0:T(1,128)} %broadcast_in_dim.88.offset, f32[4,8,1,512]{3,2,1,0:T(1,128)} %broadcast_in_dim.89.weight), custom_call_target="tpu_custom_call" | custom-call | flops 25165824 | bytes 8388608 | tf_op jit(solution)/shard_map/band/pallas_call | solution.py:70
  62.6 9.3 %mix_band.9 = (f32[4,256,256]{2,1,0:T(8,128)}, f32[4,256,256]{2,1,0:T(8,128)}) custom-call(f32[8,9]{1,0:T(8,128)} %select_add_fusion.refs_0_, f32[2,8,256,512]{3,2,1,0:T(8,128)} %refs_2_.11, f32[2,8,256,512]{3,2,1,0:T(8,128)} %refs_2_.11, f32[4,256,512]{2,1,0:T(8,128)} %collective-permute-done.2.refs_3_, bf16[8,512,512]{2,1,0:T(8,128)(2,1)} %get-tuple-element.31.refs_4_, ...), custom_call_target="tpu_custom_call" | custom-call | flops 1610612736 | bytes 12582912 | tf_op jit(solution)/shard_map/mix_band/pallas_call | solution.py:33
  72.1 9.3 %mix_band.10 = (f32[4,256,256]{2,1,0:T(8,128)}, f32[4,256,256]{2,1,0:T(8,128)}) custom-call(f32[8,9]{1,0:T(8,128)} %select_add_fusion.refs_0_, f32[4,256,512]{2,1,0:T(8,128)} %collective-permute-done.1.refs_1_, f32[2,8,256,512]{3,2,1,0:T(8,128)} %refs_2_.11, f32[2,8,256,512]{3,2,1,0:T(8,128)} %refs_2_.11, bf16[8,512,512]{2,1,0:T(8,128)(2,1)} %get-tuple-element.31.refs_4_, ...), custom_call_target="tpu_custom_call" | custom-call | flops 1610612736 | bytes 12582912 | tf_op jit(solution)/shard_map/mix_band/pallas_call | solution.py:33
  81.4 9.3 %mix_band.11 = (f32[4,256,256]{2,1,0:T(8,128)}, f32[4,256,256]{2,1,0:T(8,128)}) custom-call(f32[8,9]{1,0:T(8,128)} %select_add_fusion.refs_0_, f32[2,8,256,512]{3,2,1,0:T(8,128)} %refs_2_.11, f32[2,8,256,512]{3,2,1,0:T(8,128)} %refs_2_.11, f32[4,256,512]{2,1,0:T(8,128)} %collective-permute-done.refs_3_, bf16[8,512,512]{2,1,0:T(8,128)(2,1)} %get-tuple-element.31.refs_4_, ...), custom_call_target="tpu_custom_call" | custom-call | flops 1610612736 | bytes 12582912 | tf_op jit(solution)/shard_map/mix_band/pallas_call | solution.py:33
  90.8 6.1 %columns_band.4.refs_6_.refs_1_.refs_2_ = f32[4,512,256]{2,1,0:T(8,128)} custom-call(bf16[8,512,512]{2,1,0:T(8,128)(2,1)} %get-tuple-element.29.refs_0_.refs_4_, bf16[8,512,512]{2,1,0:T(8,128)(2,1)} %get-tuple-element.30.refs_1_.refs_5_, f32[4,256,256]{2,1,0:T(8,128)} %get-tuple-element.33.refs_6_.refs_2_, f32[4,256,256]{2,1,0:T(8,128)} %collective-permute-done.8.refs_3_, ...), custom_call_target="tpu_custom_call" | custom-call | flops 1610612736 | bytes 10485760 | tf_op jit(solution)/shard_map/columns_band/pallas_call | solution.py:33
  99.3 19.5 %collective-permute-done.6.refs_3_ = f32[4,256,256]{2,1,0:T(8,128)} collective-permute-done((f32[4,256,256]{2,1,0:T(8,128)}, f32[4,256,256]{2,1,0:T(8,128)}, u32[]{:S(2)}, u32[]{:S(2)}) %collective-permute-start.6) | collective-permute-done | bytes 1048608 | tf_op jit(solution)/shard_map/ppermute | solution.py:286
  118.8 6.2 %columns_band.5.rest_0_.refs_2_.refs_3_ = f32[4,512,256]{2,1,0:T(8,128)} custom-call(bf16[8,512,512]{2,1,0:T(8,128)(2,1)} %get-tuple-element.29.refs_0_.refs_4_, bf16[8,512,512]{2,1,0:T(8,128)(2,1)} %get-tuple-element.30.refs_1_.refs_5_, f32[4,256,256]{2,1,0:T(8,128)} %get-tuple-element.34.refs_6_.refs_2_, f32[4,256,256]{2,1,0:T(8,128)} %collective-permute-done.6.refs_3_, ...), custom_call_target="tpu_custom_call" | custom-call | flops 1610612736 | bytes 10485760 | tf_op jit(solution)/shard_map/columns_band/pallas_call | solution.py:33
  144.3 11.8 %collective-permute-done.12.refs_2_ = f32[4,256,256]{2,1,0:T(8,128)} collective-permute-done((f32[4,256,256]{2,1,0:T(8,128)}, f32[4,256,256]{2,1,0:T(8,128)}, u32[]{:S(2)}, u32[]{:S(2)}) %collective-permute-start.12) | collective-permute-done | bytes 1048608 | tf_op jit(solution)/shard_map/ppermute | solution.py:286
  158.1 20.1 %collective-permute-done.13.refs_3_ = f32[4,256,256]{2,1,0:T(8,128)} collective-permute-done((f32[4,256,256]{2,1,0:T(8,128)}, f32[4,256,256]{2,1,0:T(8,128)}, u32[]{:S(2)}, u32[]{:S(2)}) %collective-permute-start.13) | collective-permute-done | bytes 1048608 | tf_op jit(solution)/shard_map/ppermute | solution.py:286
  184.9 9.6 %mix_band.12 = (f32[4,256,256]{2,1,0:T(8,128)}, f32[4,256,256]{2,1,0:T(8,128)}) custom-call(f32[8,9]{1,0:T(8,128)} %select_add_fusion.refs_0_, f32[4,512,256]{2,1,0:T(8,128)} %columns_band.4.refs_6_.refs_1_.refs_2_, f32[4,512,256]{2,1,0:T(8,128)} %columns_band.5.rest_0_.refs_2_.refs_3_, f32[4,512,256]{2,1,0:T(8,128)} %collective-permute-done.15.refs_3_, ...), custom_call_target="tpu_custom_call" | custom-call | flops 1610612736 | bytes 12582912 | tf_op jit(solution)/shard_map/mix_band/pallas_call | solution.py:33
  194.6 6.1 %columns_band.6.refs_6_.refs_1_.refs_2_ = f32[4,512,256]{2,1,0:T(8,128)} custom-call(bf16[8,512,512]{2,1,0:T(8,128)(2,1)} %get-tuple-element.29.refs_0_.refs_4_, bf16[8,512,512]{2,1,0:T(8,128)(2,1)} %get-tuple-element.30.refs_1_.refs_5_, f32[4,256,256]{2,1,0:T(8,128)} %collective-permute-done.12.refs_2_, f32[4,256,256]{2,1,0:T(8,128)} %collective-permute-done.13.refs_3_, ...), custom_call_target="tpu_custom_call" | custom-call | flops 1610612736 | bytes 10485760 | tf_op jit(solution)/shard_map/columns_band/pallas_call | solution.py:33
  203.9 9.6 %mix_band.13 = (f32[4,256,256]{2,1,0:T(8,128)}, f32[4,256,256]{2,1,0:T(8,128)}) custom-call(f32[8,9]{1,0:T(8,128)} %select_add_fusion.refs_0_, f32[4,512,256]{2,1,0:T(8,128)} %copy-done, f32[4,512,256]{2,1,0:T(8,128)} %columns_band.4.refs_6_.refs_1_.refs_2_, f32[4,512,256]{2,1,0:T(8,128)} %columns_band.5.rest_0_.refs_2_.refs_3_, ...), custom_call_target="tpu_custom_call" | custom-call | flops 1610612736 | bytes 12582912 | tf_op jit(solution)/shard_map/mix_band/pallas_call | solution.py:33
  213.6 9.0 %collective-permute-done.5.refs_3_ = f32[4,256,256]{2,1,0:T(8,128)} collective-permute-done((f32[4,256,256]{2,1,0:T(8,128)}, f32[4,256,256]{2,1,0:T(8,128)}, u32[]{:S(2)}, u32[]{:S(2)}) %collective-permute-start.5) | collective-permute-done | bytes 1048608 | tf_op jit(solution)/shard_map/ppermute | solution.py:286
  222.6 6.5 %collective-permute-done.10.refs_5_ = f32[4,256,256]{2,1,0:T(8,128)} collective-permute-done((f32[4,256,256]{2,1,0:T(8,128)}, f32[4,256,256]{2,1,0:T(8,128)}, u32[]{:S(2)}, u32[]{:S(2)}) %collective-permute-start.10) | collective-permute-done | bytes 1048608 | tf_op jit(solution)/shard_map/ppermute | solution.py:286
  229.1 6.1 %columns_band.7.refs_2_.refs_6_.refs_3_ = f32[4,512,256]{2,1,0:T(8,128)} custom-call(bf16[8,512,512]{2,1,0:T(8,128)(2,1)} %get-tuple-element.29.refs_0_.refs_4_, bf16[8,512,512]{2,1,0:T(8,128)(2,1)} %get-tuple-element.30.refs_1_.refs_5_, f32[4,256,256]{2,1,0:T(8,128)} %collective-permute-done.4.refs_2_, f32[4,256,256]{2,1,0:T(8,128)} %collective-permute-done.5.refs_3_, ...), custom_call_target="tpu_custom_call" | custom-call | flops 1610612736 | bytes 10485760 | tf_op jit(solution)/shard_map/columns_band/pallas_call | solution.py:33
  245.2 9.7 %mix_band.14 = (f32[4,256,256]{2,1,0:T(8,128)}, f32[4,256,256]{2,1,0:T(8,128)}) custom-call(f32[8,9]{1,0:T(8,128)} %select_add_fusion.refs_0_, f32[4,512,256]{2,1,0:T(8,128)} %columns_band.6.refs_6_.refs_1_.refs_2_, f32[4,512,256]{2,1,0:T(8,128)} %columns_band.7.refs_2_.refs_6_.refs_3_, f32[4,512,256]{2,1,0:T(8,128)} %collective-permute-done.17.refs_3_, ...), custom_call_target="tpu_custom_call" | custom-call | flops 1610612736 | bytes 12582912 | tf_op jit(solution)/shard_map/mix_band/pallas_call | solution.py:33
  261.8 9.6 %mix_band.15 = (f32[4,256,256]{2,1,0:T(8,128)}, f32[4,256,256]{2,1,0:T(8,128)}) custom-call(f32[8,9]{1,0:T(8,128)} %select_add_fusion.refs_0_, f32[4,512,256]{2,1,0:T(8,128)} %copy-done.1, f32[4,512,256]{2,1,0:T(8,128)} %columns_band.6.refs_6_.refs_1_.refs_2_, f32[4,512,256]{2,1,0:T(8,128)} %columns_band.7.refs_2_.refs_6_.refs_3_, ...), custom_call_target="tpu_custom_call" | custom-call | flops 1610612736 | bytes 12582912 | tf_op jit(solution)/shard_map/mix_band/pallas_call | solution.py:33
  273.8 7.0 %band.3 = (bf16[8,512,512]{2,1,0:T(8,128)(2,1)}, bf16[8,512,512]{2,1,0:T(8,128)(2,1)}) custom-call(s32[2]{0:T(128)} %pad_add_fusion.2.bases, s32[8,1,512]{2,1,0:T(1,128)} %broadcast_in_dim.75.offset, f32[4,8,1,512]{3,2,1,0:T(1,128)} %broadcast_in_dim.76.weight), custom_call_target="tpu_custom_call" | custom-call | flops 25165824 | bytes 8388608 | tf_op jit(solution)/shard_map/band/pallas_call | solution.py:70
  292.7 15.7 %collective-permute-done.20.refs_3_ = f32[4,256,256]{2,1,0:T(8,128)} collective-permute-done((f32[4,256,256]{2,1,0:T(8,128)}, f32[4,256,256]{2,1,0:T(8,128)}, u32[]{:S(2)}, u32[]{:S(2)}) %collective-permute-start.20) | collective-permute-done | bytes 1048608 | tf_op jit(solution)/shard_map/ppermute | solution.py:286
  308.4 23.2 %collective-permute-done.21.refs_4_ = f32[4,256,256]{2,1,0:T(8,128)} collective-permute-done((f32[4,256,256]{2,1,0:T(8,128)}, f32[4,256,256]{2,1,0:T(8,128)}, u32[]{:S(2)}, u32[]{:S(2)}) %collective-permute-start.21) | collective-permute-done | bytes 1048608 | tf_op jit(solution)/shard_map/ppermute | solution.py:286
  337.7 6.1 %last_rows.6.refs_5_ = f32[2,8,256,512]{3,2,1,0:T(8,128)} custom-call(bf16[8,512,512]{2,1,0:T(8,128)(2,1)} %get-tuple-element.27.refs_0_, bf16[8,512,512]{2,1,0:T(8,128)(2,1)} %get-tuple-element.28.refs_1_, f32[2,8,256,512]{3,2,1,0:T(8,128)} %refs_2_.15, f32[4,256,256]{2,1,0:T(8,128)} %get-tuple-element.43.refs_6_.refs_3_, ...), custom_call_target="tpu_custom_call", output_to_operand_aliasing={{}: (5, {})} | custom-call | flops 1610612736 | bytes 10485760 | tf_op jit(solution)/shard_map/last_rows/pallas_call | solution.py:33
  (95 shorter events, 115.3 us)
Async XLA Ops:
  6.6 32.6 %collective-permute-start.3 = (f32[4,256,512]{2,1,0:T(8,128)}, f32[4,256,512]{2,1,0:T(8,128)}, u32[]{:S(2)}, u32[]{:S(2)}) collective-permute-start(f32[4,256,512]{2,1,0:T(8,128)} %get-tuple-element.49), channel_id=1, source_target_pairs={{0,4},{4,8},{8,12},{1,5},{5,9},{9,13},{2,6},{6,10},{10,14},{3,7},{... | collective-permute-start | bytes 6291464 | tf_op jit(solution)/shard_map/ppermute | solution.py:278
  10.2 51.0 %collective-permute-start.2 = (f32[4,256,512]{2,1,0:T(8,128)}, f32[4,256,512]{2,1,0:T(8,128)}, u32[]{:S(2)}, u32[]{:S(2)}) collective-permute-start(f32[4,256,512]{2,1,0:T(8,128)} %get-tuple-element.50), channel_id=1, source_target_pairs={{4,0},{8,4},{12,8},{5,1},{9,5},{13,9},{6,2},{10,6},{14,10},{7,3},{... | collective-permute-start | bytes 6291464 | tf_op jit(solution)/shard_map/ppermute | solution.py:278
  12.2 59.6 %collective-permute-start.1 = (f32[4,256,512]{2,1,0:T(8,128)}, f32[4,256,512]{2,1,0:T(8,128)}, u32[]{:S(2)}, u32[]{:S(2)}) collective-permute-start(f32[4,256,512]{2,1,0:T(8,128)} %get-tuple-element.51), channel_id=1, source_target_pairs={{0,4},{4,8},{8,12},{1,5},{5,9},{9,13},{2,6},{6,10},{10,14},{3,7},{... | collective-permute-start | bytes 6291464 | tf_op jit(solution)/shard_map/ppermute | solution.py:278
  15.8 65.6 %collective-permute-start = (f32[4,256,512]{2,1,0:T(8,128)S(1)}, f32[4,256,512]{2,1,0:T(8,128)}, u32[]{:S(2)}, u32[]{:S(2)}) collective-permute-start(f32[4,256,512]{2,1,0:T(8,128)S(1)} %get-tuple-element.52), channel_id=1, source_target_pairs={{4,0},{8,4},{12,8},{5,1},{9,5},{13,9},{6,2},{10,6},{14,10},{7,3},{... | collective-permute-start | bytes 6291464 | tf_op jit(solution)/shard_map/ppermute | solution.py:278
  21.3 69.4 %collective-permute-start.9 = (f32[4,256,256]{2,1,0:T(8,128)}, f32[4,256,256]{2,1,0:T(8,128)}, u32[]{:S(2)}, u32[]{:S(2)}) collective-permute-start(f32[4,256,256]{2,1,0:T(8,128)} %take.11), channel_id=1, source_target_pairs={{0,16},{1,17},{2,18},{3,19},{16,0},{17,1},{18,2},{19,3},{4,20},{5,... | collective-permute-start | bytes 3145736 | tf_op jit(solution)/shard_map/ppermute | solution.py:286
  48.4 42.3 %collective-permute-start.8 = (f32[4,256,256]{2,1,0:T(8,128)}, f32[4,256,256]{2,1,0:T(8,128)}, u32[]{:S(2)}, u32[]{:S(2)}) collective-permute-start(f32[4,256,256]{2,1,0:T(8,128)} %get-tuple-element.39), channel_id=1, source_target_pairs={{0,16},{1,17},{2,18},{3,19},{16,0},{17,1},{18,2},{19,3},{4,20},{5,... | collective-permute-start | bytes 3145736 | tf_op jit(solution)/shard_map/ppermute | solution.py:286
  61.3 38.0 %collective-permute-start.7 = (f32[4,256,256]{2,1,0:T(8,128)}, f32[4,256,256]{2,1,0:T(8,128)S(1)}, u32[]{:S(2)}, u32[]{:S(2)}) collective-permute-start(f32[4,256,256]{2,1,0:T(8,128)} %take.10), channel_id=1, source_target_pairs={{0,16},{1,17},{2,18},{3,19},{16,0},{17,1},{18,2},{19,3},{4,20},{5,... | collective-permute-start | bytes 3145736 | tf_op jit(solution)/shard_map/ppermute | solution.py:286
  71.9 47.0 %collective-permute-start.6 = (f32[4,256,256]{2,1,0:T(8,128)}, f32[4,256,256]{2,1,0:T(8,128)}, u32[]{:S(2)}, u32[]{:S(2)}) collective-permute-start(f32[4,256,256]{2,1,0:T(8,128)} %get-tuple-element.38), channel_id=1, source_target_pairs={{0,16},{1,17},{2,18},{3,19},{16,0},{17,1},{18,2},{19,3},{4,20},{5,... | collective-permute-start | bytes 3145736 | tf_op jit(solution)/shard_map/ppermute | solution.py:286
  96.9 84.3 %collective-permute-start.15 = (f32[4,512,256]{2,1,0:T(8,128)}, f32[4,512,256]{2,1,0:T(8,128)}, u32[]{:S(2)}, u32[]{:S(2)}) collective-permute-start(f32[4,512,256]{2,1,0:T(8,128)} %columns_band.4.refs_6_.refs_1_.refs_2_), channel_id=1, source_target_pairs={{4,0},{8,4},{12,8},{5,1},{9,5},{13,9},{6,2},{10,6},{14,10},{7,3},{... | collective-permute-start | bytes 6291464 | tf_op jit(solution)/shard_map/ppermute | solution.py:278
  125.0 77.6 %collective-permute-start.11 = (f32[4,512,256]{2,1,0:T(8,128)}, f32[4,512,256]{2,1,0:T(8,128)S(1)}, u32[]{:S(2)}, u32[]{:S(2)}) collective-permute-start(f32[4,512,256]{2,1,0:T(8,128)} %columns_band.5.rest_0_.refs_2_.refs_3_), channel_id=1, source_target_pairs={{0,4},{4,8},{8,12},{1,5},{5,9},{9,13},{2,6},{6,10},{10,14},{3,7},{... | collective-permute-start | bytes 6291464 | tf_op jit(solution)/shard_map/ppermute | solution.py:278
  128.7 27.3 %collective-permute-start.12 = (f32[4,256,256]{2,1,0:T(8,128)}, f32[4,256,256]{2,1,0:T(8,128)}, u32[]{:S(2)}, u32[]{:S(2)}) collective-permute-start(f32[4,256,256]{2,1,0:T(8,128)} %get-tuple-element.35.refs_6_), channel_id=1, source_target_pairs={{1,0},{2,1},{3,2},{17,16},{18,17},{19,18},{5,4},{6,5},{7,6},{21,20... | collective-permute-start | bytes 3145736 | tf_op jit(solution)/shard_map/ppermute | solution.py:286
  130.8 47.4 %collective-permute-start.13 = (f32[4,256,256]{2,1,0:T(8,128)}, f32[4,256,256]{2,1,0:T(8,128)}, u32[]{:S(2)}, u32[]{:S(2)}) collective-permute-start(f32[4,256,256]{2,1,0:T(8,128)} %get-tuple-element.40), channel_id=1, source_target_pairs={{1,16},{2,17},{3,18},{17,0},{18,1},{19,2},{5,20},{6,21},{7,22},{21... | collective-permute-start | bytes 3145736 | tf_op jit(solution)/shard_map/ppermute | solution.py:286
  136.2 58.4 %collective-permute-start.14 = (f32[4,256,256]{2,1,0:T(8,128)}, f32[4,256,256]{2,1,0:T(8,128)}, u32[]{:S(2)}, u32[]{:S(2)}) collective-permute-start(f32[4,256,256]{2,1,0:T(8,128)} %take.15), channel_id=1, source_target_pairs={{0,16},{1,17},{2,18},{3,19},{16,0},{17,1},{18,2},{19,3},{4,20},{5,... | collective-permute-start | bytes 3145736 | tf_op jit(solution)/shard_map/ppermute | solution.py:286
  156.0 57.5 %collective-permute-start.4 = (f32[4,256,256]{2,1,0:T(8,128)S(1)}, f32[4,256,256]{2,1,0:T(8,128)}, u32[]{:S(2)}, u32[]{:S(2)}) collective-permute-start(f32[4,256,256]{2,1,0:T(8,128)S(1)} %copy-done.5), channel_id=1, source_target_pairs={{1,0},{2,1},{3,2},{17,16},{18,17},{19,18},{5,4},{6,5},{7,6},{21,20... | collective-permute-start | bytes 3145736 | tf_op jit(solution)/shard_map/ppermute | solution.py:286
  178.2 44.4 %collective-permute-start.5 = (f32[4,256,256]{2,1,0:T(8,128)}, f32[4,256,256]{2,1,0:T(8,128)}, u32[]{:S(2)}, u32[]{:S(2)}) collective-permute-start(f32[4,256,256]{2,1,0:T(8,128)} %get-tuple-element.37), channel_id=1, source_target_pairs={{1,16},{2,17},{3,18},{17,0},{18,1},{19,2},{5,20},{6,21},{7,22},{21... | collective-permute-start | bytes 3145736 | tf_op jit(solution)/shard_map/ppermute | solution.py:286
  181.2 47.8 %collective-permute-start.10 = (f32[4,256,256]{2,1,0:T(8,128)}, f32[4,256,256]{2,1,0:T(8,128)}, u32[]{:S(2)}, u32[]{:S(2)}) collective-permute-start(f32[4,256,256]{2,1,0:T(8,128)} %take.14), channel_id=1, source_target_pairs={{0,16},{1,17},{2,18},{3,19},{16,0},{17,1},{18,2},{19,3},{4,20},{5,... | collective-permute-start | bytes 3145736 | tf_op jit(solution)/shard_map/ppermute | solution.py:286
  200.7 42.4 %collective-permute-start.17 = (f32[4,512,256]{2,1,0:T(8,128)}, f32[4,512,256]{2,1,0:T(8,128)}, u32[]{:S(2)}, u32[]{:S(2)}) collective-permute-start(f32[4,512,256]{2,1,0:T(8,128)} %columns_band.6.refs_6_.refs_1_.refs_2_), channel_id=1, source_target_pairs={{4,0},{8,4},{12,8},{5,1},{9,5},{13,9},{6,2},{10,6},{14,10},{7,3},{... | collective-permute-start | bytes 6291464 | tf_op jit(solution)/shard_map/ppermute | solution.py:278
  235.2 25.2 %collective-permute-start.16 = (f32[4,512,256]{2,1,0:T(8,128)}, f32[4,512,256]{2,1,0:T(8,128)S(1)}, u32[]{:S(2)}, u32[]{:S(2)}) collective-permute-start(f32[4,512,256]{2,1,0:T(8,128)} %columns_band.7.refs_2_.refs_6_.refs_3_), channel_id=1, source_target_pairs={{0,4},{4,8},{8,12},{1,5},{5,9},{9,13},{2,6},{6,10},{10,14},{3,7},{... | collective-permute-start | bytes 6291464 | tf_op jit(solution)/shard_map/ppermute | solution.py:278
  237.1 34.3 %collective-permute-start.22 = (f32[4,256,256]{2,1,0:T(8,128)}, f32[4,256,256]{2,1,0:T(8,128)S(1)}, u32[]{:S(2)}, u32[]{:S(2)}) collective-permute-start(f32[4,256,256]{2,1,0:T(8,128)} %get-tuple-element.41.refs_6_), channel_id=1, source_target_pairs={{1,0},{2,1},{3,2},{17,16},{18,17},{19,18},{5,4},{6,5},{7,6},{21,20... | collective-permute-start | bytes 3145736 | tf_op jit(solution)/shard_map/ppermute | solution.py:286
  239.2 47.4 %collective-permute-start.23 = (f32[4,256,256]{2,1,0:T(8,128)}, f32[4,256,256]{2,1,0:T(8,128)}, u32[]{:S(2)}, u32[]{:S(2)}) collective-permute-start(f32[4,256,256]{2,1,0:T(8,128)} %get-tuple-element.48), channel_id=1, source_target_pairs={{1,16},{2,17},{3,18},{17,0},{18,1},{19,2},{5,20},{6,21},{7,22},{21... | collective-permute-start | bytes 3145736 | tf_op jit(solution)/shard_map/ppermute | solution.py:286
  241.2 67.2 %collective-permute-start.20 = (f32[4,256,256]{2,1,0:T(8,128)}, f32[4,256,256]{2,1,0:T(8,128)}, u32[]{:S(2)}, u32[]{:S(2)}) collective-permute-start(f32[4,256,256]{2,1,0:T(8,128)} %get-tuple-element.42.refs_6_), channel_id=1, source_target_pairs={{1,0},{2,1},{3,2},{17,16},{18,17},{19,18},{5,4},{6,5},{7,6},{21,20... | collective-permute-start | bytes 3145736 | tf_op jit(solution)/shard_map/ppermute | solution.py:286
  243.1 88.5 %collective-permute-start.21 = (f32[4,256,256]{2,1,0:T(8,128)}, f32[4,256,256]{2,1,0:T(8,128)}, u32[]{:S(2)}, u32[]{:S(2)}) collective-permute-start(f32[4,256,256]{2,1,0:T(8,128)} %get-tuple-element.47), channel_id=1, source_target_pairs={{1,16},{2,17},{3,18},{17,0},{18,1},{19,2},{5,20},{6,21},{7,22},{21... | collective-permute-start | bytes 3145736 | tf_op jit(solution)/shard_map/ppermute | solution.py:286
  260.4 77.3 %collective-permute-start.19 = (f32[4,256,256]{2,1,0:T(8,128)}, f32[4,256,256]{2,1,0:T(8,128)}, u32[]{:S(2)}, u32[]{:S(2)}) collective-permute-start(f32[4,256,256]{2,1,0:T(8,128)} %get-tuple-element.46), channel_id=1, source_target_pairs={{0,16},{1,17},{2,18},{3,19},{16,0},{17,1},{18,2},{19,3},{4,20},{5,... | collective-permute-start | bytes 3145736 | tf_op jit(solution)/shard_map/ppermute | solution.py:286
  271.4 77.4 %collective-permute-start.18 = (f32[4,256,256]{2,1,0:T(8,128)}, f32[4,256,256]{2,1,0:T(8,128)S(1)}, u32[]{:S(2)}, u32[]{:S(2)}) collective-permute-start(f32[4,256,256]{2,1,0:T(8,128)} %get-tuple-element.45), channel_id=1, source_target_pairs={{0,16},{1,17},{2,18},{3,19},{16,0},{17,1},{18,2},{19,3},{4,20},{5,... | collective-permute-start | bytes 3145736 | tf_op jit(solution)/shard_map/ppermute | solution.py:286
  (12 other events, 89.6 us)

commit v3 on v2

--- a/solution.py
+++ b/solution.py
@@ -12,6 +12,7 @@
 DISCOUNT = 0.96
 SPAN = 2 * REACH + 1
 VMEM_BYTES = 60 * 1024 * 1024
+HINT = pl.CostEstimate(flops=1024, bytes_accessed=1024, transcendentals=0)
 
 
 def params():
@@ -79,9 +80,7 @@
         out_specs=(spec, spec),
         scratch_shapes=[pltpu.VMEM((extent, extent), jnp.float32)],
         compiler_params=params(),
-        cost_estimate=pl.CostEstimate(
-            flops=states * extent * extent * 12, bytes_accessed=states * extent * extent * 4, transcendentals=0
-        ),
+        cost_estimate=HINT,
         name="band",
     )(bases, offset[:, None, :], weight[:, :, None, :])
 
@@ -114,7 +113,7 @@
             copies[number + SPAN - 1].wait()
 
     rows = xh.shape[0]
-    step = 16
+    step = min(rows, 16 * 1024 // xh.shape[1])
     shares = [mixing[base + e, d] for d in range(SPAN)]
 
     def chunk(i, carry):
@@ -125,7 +124,7 @@
         xh[at, :], xl[at, :] = halves(total)
         return carry
 
-    lax.fori_loop(0, rows // step, chunk, 0)
+    lax.fori_loop(0, rows // step, chunk, 0, unroll=2 if rows // step % 2 == 0 else 1)
     if left_product:
         result = dot3(high[0], low[0], xh[...], xl[...])
         width = result.shape[0] // pieces
@@ -161,11 +160,7 @@
             pltpu.VMEM((rows, columns), jnp.bfloat16),
             pltpu.SemaphoreType.DMA((3 * quad,)),
         ],
-        cost_estimate=pl.CostEstimate(
-            flops=quad * rows * columns * extent * 6,
-            bytes_accessed=4 * quad * rows * columns * 4 + 4 * quad * extent * extent,
-            transcendentals=0,
-        ),
+        cost_estimate=HINT,
         name="mix_band",
     )(mixing, *arrays, *pair)
 
@@ -196,11 +191,7 @@
         in_specs=[matrix] * 2 + [piece] * (2 * pieces),
         out_specs=pl.BlockSpec((1, extent, columns), lambda e: (e, 0, 0)),
         scratch_shapes=[pltpu.VMEM((extent, columns), jnp.bfloat16)] * 2,
-        cost_estimate=pl.CostEstimate(
-            flops=quad * extent * columns * extent * 6,
-            bytes_accessed=3 * quad * extent * columns * 4 + 4 * quad * extent * extent,
-            transcendentals=0,
-        ),
+        cost_estimate=HINT,
         name="columns_band",
     )(*pair, *parts, *flows)
 
@@ -237,11 +228,7 @@
         in_specs=[matrix] * 2 + [flow] + [piece] * pieces + [pl.BlockSpec(memory_space=pl.ANY)] * len(before),
         out_specs=flow,
         input_output_aliases={} if whole is None else {3 + pieces: 0},
-        cost_estimate=pl.CostEstimate(
-            flops=quad * rows * extent * extent * 6,
-            bytes_accessed=3 * quad * rows * extent * 4 + 4 * quad * extent * extent,
-            transcendentals=0,
-        ),
+        cost_estimate=HINT,
         name="last_rows",
     )(*pair, utility, *parts, *before)
 
@@ -266,9 +253,7 @@
             out_specs=pl.BlockSpec((1, rows, columns), lambda e, place: (e, 0, 0)),
         ),
         compiler_params=params(),
-        cost_estimate=pl.CostEstimate(
-            flops=0, bytes_accessed=2 * quad * rows * columns * 4, transcendentals=0
-        ),
+        cost_estimate=HINT,
         name="take",
     )(jnp.reshape(jnp.asarray(block, jnp.int32), (1,)), utility, *after)
 
@@ -352,17 +337,23 @@
         slot = support_start + number - own + REACH
         mixing = mixing + jnp.where(slots[None, :] == slot[:, None], shares[number][:, None], 0.0)
 
-    def first_half(age, by, after):
+    def first_half(age, by, after, between):
         left = shifted(values[age, quad:], "earn", 1)
         right = shifted(values[age, :quad], "earn", -1)
         head, tail = (values, age, 0), (values, age, quad)
         parts = [mixed_product((left, head, tail), mixing, liquid_first, 0, False, count, after)]
-        parts.append(mixed_product((head, tail, right), mixing, liquid_first, quad, False, count, (parts[0][0],)))
+        parts.append(mixed_product((head, tail, right), mixing, liquid_first, quad, False, count, (parts[0][0],) + between))
         return parts[1][0], [exchanged(part, by) for part in parts]
 
     def flow_columns(age, i, after):
-        parts = [taken_columns(utility, age, i * quad, block, columns, after) for block in ahead]
-        return parts[0], exchanged(parts)
+        away = [taken_columns(utility, age, i * quad, block, columns, after) for block in ahead[1:]]
+
+        sent = exchanged([away[-1]] + away)[1:]
+
+        def with_own(stays):
+            return [taken_columns(utility, age, i * quad, me, columns, stays)] + sent
+
+        return away[-1], sent[-1], with_own
 
     def middle(arrived, flows, i, after):
         return column_product(arrived[i], flows[i], illiquid_first, i * quad, after)
@@ -370,36 +361,36 @@
     def second_half(sides, i, after):
         return mixed_product(sides, mixing, illiquid_second, i * quad, True, count, after)
 
-    done, flow_a = zip(*[flow_columns(0, i, ()) for i in range(2)])
-    done, arrived_a = first_half(1, 0, tuple(done))
-    done, arrived_b = first_half(0, -1, (done,))
-
-    head_a = middle(arrived_a, flow_a, 0, (done,))
+    first, came_0, own_a0 = flow_columns(0, 0, ())
+    second, came_1, own_a1 = flow_columns(0, 1, (first,))
+    done, arrived_a = first_half(1, 0, (came_0,), ())
+    flow_a = (own_a0((done,)), own_a1((done,)))
+    done, arrived_b = first_half(0, -1, (done, came_1), ())
+    first, came_0, own_b0 = flow_columns(1, 0, (done,))
+    second, came_1, own_b1 = flow_columns(1, 1, (first,))
+
+    head_a = middle(arrived_a, flow_a, 0, (second,))
     right_a = shifted(head_a, "earn", -1)
-    tail_a = middle(arrived_a, flow_a, 1, (head_a,))
+    flow_b = (own_b0((head_a,)), own_b1((head_a,)))
+    tail_a = middle(arrived_a, flow_a, 1, (flow_b[1][0], came_0, came_1, *arrived_b[0], *arrived_b[1]))
     left_a = shifted(tail_a, "earn", 1)
-    first, flow_b0 = flow_columns(1, 0, (tail_a,))
-    second, flow_b1 = flow_columns(1, 1, (first,))
-    flow_b = (flow_b0, flow_b1)
-
-    parts = second_half((head_a, tail_a, right_a), 1, (second,))
+    tail_b = middle(arrived_b, flow_b, 1, (tail_a,))
+    left_b = shifted(tail_b, "earn", 1)
+    head_b = middle(arrived_b, flow_b, 0, (tail_b,))
+    right_b = shifted(head_b, "earn", -1)
+
+    parts = second_half((head_a, tail_a, right_a), 1, (head_b,))
     last_a1 = exchanged(parts, -1)
-    head_b = middle(arrived_b, flow_b, 0, (parts[0],))
-    right_b = shifted(head_b, "earn", -1)
-    parts = second_half((left_a, head_a, tail_a), 0, (head_b,))
+    parts = second_half((left_a, head_a, tail_a), 0, (parts[0],))
     last_a0 = exchanged(parts, -1)
-    tail_b = middle(arrived_b, flow_b, 1, (parts[0],))
-    left_b = shifted(tail_b, "earn", 1)
-
-    parts = second_half((head_b, tail_b, right_b), 1, (tail_b,))
-    last_b1 = exchanged(parts)
     parts = second_half((left_b, head_b, tail_b), 0, (parts[0],))
     last_b0 = exchanged(parts)
-
+    parts = second_half((head_b, tail_b, right_b), 1, (parts[0],))
+    last_b1 = exchanged(parts)
     whole = last_rows(last_a1, liquid_second, quad, utility, 1, None, (parts[0],))
     whole = last_rows(last_a0, liquid_second, 0, utility, 1, whole)
-    whole = last_rows(last_b1, liquid_second, quad, utility, 0, whole)
-    return last_rows(last_b0, liquid_second, 0, utility, 0, whole)
+    whole = last_rows(last_b0, liquid_second, 0, utility, 0, whole)
+    return last_rows(last_b1, liquid_second, quad, utility, 0, whole)
 
 
 def solution(mesh):

time: 359 us -> 370 us (1.031)
  waiting for transfers between devices: 122 us -> 137 us
  Pallas kernels: 173 us -> 168 us
    ppermute x16, waiting for transfers between devices: 117 us -> 133 us  [exchanged(): lax.ppermute(piece, ('asset', 'age'), [(a * ages + z, (a + s) % count * a...]
    pallas_call x16, Pallas kernels: 125 us -> 120 us  [ordered_call(): return lambda *operands: call(*operands, *after)]
  transfers between devices with their start and end apart: 24 -> 24, of which waited for: 10 -> 11; matrix products, arithmetic and copies ran while one was open for 2% -> 3% of each run, Pallas kernels for 47% -> 43%
where the time goes in v3:
time: 370 us; the launch traced here: 367 us
  Pallas kernels  168 us (45%)
  waiting for transfers between devices  137 us (37%)
  starting transfers between devices  46 us (12%)
  local copies, waits for them, and re-layouts  12.6 us (3%)
    ppermute x16, waiting for transfers between devices, exchanged(): lax.ppermute(piece, ('asset', 'age'), [(a * ages + z, (a + s) % count * a...  133 us
    pallas_call x16, Pallas kernels, ordered_call(): return lambda *operands: call(*operands, *after)  120 us
    pallas_call x8, Pallas kernels, taken_columns(): pl.pallas_call(lambda place, flow, *rest: take_kernel(place, flow, rest[-...  27.1 us
    ppermute x16, starting transfers between devices, exchanged(): lax.ppermute(piece, ('asset', 'age'), [(a * ages + z, (a + s) % count * a...  23.7 us
    ppermute x8, starting transfers between devices, shifted(): lax.ppermute(value, axis, [(i, i + by) for i in range(count) if 0 <= i +...  22.3 us
    pallas_call x3, Pallas kernels, band_pair(): pl.pallas_call(functools.partial(band_kernel, flip), grid=(states,), out_...  21.2 us
  transfers between devices with their start and end apart: 24, of which 11 were waited for; matrix products, arithmetic and copies ran while one was open for 3% of the time, Pallas kernels for 43%

profile of v3, /device:TPU:17, one launch (start us, length us, event | category | flops | bytes accessed | tf_op | source)
XLA Modules:
  0.0 366.6 jit_solution(15371037571423312620)
XLA Ops:
  4.6 6.9 %slice_bitcast_fusion = (f32[4,256,512]{2,1,0:T(8,128)}, f32[4,256,512]{2,1,0:T(8,128)}, f32[4,256,512]{2,1,0:T(8,128)}, f32[4,256,512]{2,1,0:T(8,128)}) fusion(f32[2,8,256,512]{3,2,1,0:T(8,128)} %refs_2_.11), kind=kLoop, calls=%fused_computation | loop fusion | bytes 16777216 | tf_op jit(solution)/shard_map/squeeze | solution.py:342
  30.7 6.9 %band.5 = (bf16[8,512,512]{2,1,0:T(8,128)(2,1)}, bf16[8,512,512]{2,1,0:T(8,128)(2,1)}) custom-call(s32[2]{0:T(128)} %iota_multiply_fusion.bases, s32[8,1,512]{2,1,0:T(1,128)} %broadcast_in_dim.90.offset, f32[4,8,1,512]{3,2,1,0:T(1,128)} %broadcast_in_dim.91.weight), custom_call_target="tpu_custom_call" | custom-call | flops 1024 | bytes 1024 | tf_op jit(solution)/shard_map/band/pallas_call | solution.py:71
  38.8 8.9 %mix_band.8 = (f32[4,256,256]{2,1,0:T(8,128)}, f32[4,256,256]{2,1,0:T(8,128)}) custom-call(f32[8,9]{1,0:T(8,128)} %select_add_fusion.refs_0_, f32[4,256,512]{2,1,0:T(8,128)} %collective-permute-done.2.refs_1_, f32[2,8,256,512]{3,2,1,0:T(8,128)} %refs_2_.11, f32[2,8,256,512]{3,2,1,0:T(8,128)} %refs_2_.11, bf16[8,512,512]{2,1,0:T(8,128)(2,1)} %get-tuple-element.31.refs_4_, ...), custom_call_target="tpu_custom_call" | custom-call | flops 1024 | bytes 1024 | tf_op jit(solution)/shard_map/mix_band/pallas_call | solution.py:34
  48.0 8.9 %mix_band.9 = (f32[4,256,256]{2,1,0:T(8,128)}, f32[4,256,256]{2,1,0:T(8,128)}) custom-call(f32[8,9]{1,0:T(8,128)} %select_add_fusion.refs_0_, f32[2,8,256,512]{3,2,1,0:T(8,128)} %refs_2_.11, f32[2,8,256,512]{3,2,1,0:T(8,128)} %refs_2_.11, f32[4,256,512]{2,1,0:T(8,128)} %collective-permute-done.1.refs_3_, bf16[8,512,512]{2,1,0:T(8,128)(2,1)} %get-tuple-element.31.refs_4_, ...), custom_call_target="tpu_custom_call" | custom-call | flops 1024 | bytes 1024 | tf_op jit(solution)/shard_map/mix_band/pallas_call | solution.py:34
  61.2 8.9 %mix_band.10 = (f32[4,256,256]{2,1,0:T(8,128)}, f32[4,256,256]{2,1,0:T(8,128)}) custom-call(f32[8,9]{1,0:T(8,128)} %select_add_fusion.refs_0_, f32[4,256,512]{2,1,0:T(8,128)} %collective-permute-done.refs_1_, f32[2,8,256,512]{3,2,1,0:T(8,128)} %refs_2_.11, f32[2,8,256,512]{3,2,1,0:T(8,128)} %refs_2_.11, bf16[8,512,512]{2,1,0:T(8,128)(2,1)} %get-tuple-element.31.refs_4_, ...), custom_call_target="tpu_custom_call" | custom-call | flops 1024 | bytes 1024 | tf_op jit(solution)/shard_map/mix_band/pallas_call | solution.py:34
  70.2 9.0 %mix_band.11 = (f32[4,256,256]{2,1,0:T(8,128)}, f32[4,256,256]{2,1,0:T(8,128)}) custom-call(f32[8,9]{1,0:T(8,128)} %select_add_fusion.refs_0_, f32[2,8,256,512]{3,2,1,0:T(8,128)} %refs_2_.11, f32[2,8,256,512]{3,2,1,0:T(8,128)} %refs_2_.11, f32[4,256,512]{2,1,0:T(8,128)} %collective-permute-done.8.refs_3_, bf16[8,512,512]{2,1,0:T(8,128)(2,1)} %get-tuple-element.31.refs_4_, ...), custom_call_target="tpu_custom_call" | custom-call | flops 1024 | bytes 1024 | tf_op jit(solution)/shard_map/mix_band/pallas_call | solution.py:34
  93.5 17.8 %collective-permute-done.12.refs_8_.refs_5_ = f32[4,256,256]{2,1,0:T(8,128)S(1)} collective-permute-done((f32[4,256,256]{2,1,0:T(8,128)}, f32[4,256,256]{2,1,0:T(8,128)S(1)}, u32[]{:S(2)}, u32[]{:S(2)}) %collective-permute-start.12) | collective-permute-done | bytes 1048608 | tf_op jit(solution)/shard_map/ppermute | solution.py:271
  113.3 19.5 %collective-permute-done.9.refs_7_.refs_5_ = f32[4,256,256]{2,1,0:T(8,128)S(1)} collective-permute-done((f32[4,256,256]{2,1,0:T(8,128)}, f32[4,256,256]{2,1,0:T(8,128)S(1)}, u32[]{:S(2)}, u32[]{:S(2)}) %collective-permute-start.9) | collective-permute-done | bytes 1048608 | tf_op jit(solution)/shard_map/ppermute | solution.py:271
  135.9 7.3 %band.4 = (bf16[8,512,512]{2,1,0:T(8,128)(2,1)}, bf16[8,512,512]{2,1,0:T(8,128)(2,1)}) custom-call(s32[2]{0:T(128)} %pad_add_fusion.2.bases, s32[8,1,512]{2,1,0:T(1,128)} %broadcast_in_dim.88.offset, f32[4,8,1,512]{3,2,1,0:T(1,128)} %broadcast_in_dim.89.weight), custom_call_target="tpu_custom_call" | custom-call | flops 1024 | bytes 1024 | tf_op jit(solution)/shard_map/band/pallas_call | solution.py:71
  146.6 6.1 %columns_band.4.rest_0_.refs_1_.refs_2_ = f32[4,512,256]{2,1,0:T(8,128)} custom-call(bf16[8,512,512]{2,1,0:T(8,128)(2,1)} %get-tuple-element.29.refs_0_.refs_4_, bf16[8,512,512]{2,1,0:T(8,128)(2,1)} %get-tuple-element.30.refs_1_.refs_5_, f32[4,256,256]{2,1,0:T(8,128)} %get-tuple-element.33.refs_6_.refs_2_, f32[4,256,256]{2,1,0:T(8,128)} %collective-permute-done.7.refs_3_, ...), custom_call_target="tpu_custom_call" | custom-call | flops 1024 | bytes 1024 | tf_op jit(solution)/shard_map/columns_band/pallas_call | solution.py:34
  162.0 19.8 %collective-permute-done.6.refs_10_.refs_3_ = f32[4,256,256]{2,1,0:T(8,128)} collective-permute-done((f32[4,256,256]{2,1,0:T(8,128)}, f32[4,256,256]{2,1,0:T(8,128)}, u32[]{:S(2)}, u32[]{:S(2)}) %collective-permute-start.6) | collective-permute-done | bytes 1048608 | tf_op jit(solution)/shard_map/ppermute | solution.py:271
  181.7 21.3 %collective-permute-done.13.refs_3_ = f32[4,256,256]{2,1,0:T(8,128)} collective-permute-done((f32[4,256,256]{2,1,0:T(8,128)}, f32[4,256,256]{2,1,0:T(8,128)}, u32[]{:S(2)}, u32[]{:S(2)}) %collective-permute-start.13) | collective-permute-done | bytes 1048608 | tf_op jit(solution)/shard_map/ppermute | solution.py:271
  203.0 6.2 %columns_band.5.refs_6_.refs_2_.refs_3_ = f32[4,512,256]{2,1,0:T(8,128)} custom-call(bf16[8,512,512]{2,1,0:T(8,128)(2,1)} %get-tuple-element.29.refs_0_.refs_4_, bf16[8,512,512]{2,1,0:T(8,128)(2,1)} %get-tuple-element.30.refs_1_.refs_5_, f32[4,256,256]{2,1,0:T(8,128)} %get-tuple-element.34.refs_6_.rest_0_.refs_2_, ...), custom_call_target="tpu_custom_call" | custom-call | flops 1024 | bytes 1024 | tf_op jit(solution)/shard_map/columns_band/pallas_call | solution.py:34
  211.1 6.2 %columns_band.6.refs_6_.refs_3_.refs_2_ = f32[4,512,256]{2,1,0:T(8,128)} custom-call(bf16[8,512,512]{2,1,0:T(8,128)(2,1)} %get-tuple-element.29.refs_0_.refs_4_, bf16[8,512,512]{2,1,0:T(8,128)(2,1)} %get-tuple-element.30.refs_1_.refs_5_, f32[4,256,256]{2,1,0:T(8,128)} %copy-done.3, f32[4,256,256]{2,1,0:T(8,128)} %collective-permute-done.11.refs_12_.refs_3_, ...), custom_call_target="tpu_custom_call" | custom-call | flops 1024 | bytes 1024 | tf_op jit(solution)/shard_map/columns_band/pallas_call | solution.py:34
  222.6 6.1 %columns_band.7.refs_6_.refs_2_.refs_1_ = f32[4,512,256]{2,1,0:T(8,128)} custom-call(bf16[8,512,512]{2,1,0:T(8,128)(2,1)} %get-tuple-element.29.refs_0_.refs_4_, bf16[8,512,512]{2,1,0:T(8,128)(2,1)} %get-tuple-element.30.refs_1_.refs_5_, f32[4,256,256]{2,1,0:T(8,128)} %collective-permute-done.5.refs_9_.refs_2_, ...), custom_call_target="tpu_custom_call" | custom-call | flops 1024 | bytes 1024 | tf_op jit(solution)/shard_map/columns_band/pallas_call | solution.py:34
  233.1 8.8 %mix_band.12 = (f32[4,256,256]{2,1,0:T(8,128)}, f32[4,256,256]{2,1,0:T(8,128)}) custom-call(f32[8,9]{1,0:T(8,128)} %select_add_fusion.refs_0_, f32[4,512,256]{2,1,0:T(8,128)} %columns_band.4.rest_0_.refs_1_.refs_2_, f32[4,512,256]{2,1,0:T(8,128)} %columns_band.5.refs_6_.refs_2_.refs_3_, f32[4,512,256]{2,1,0:T(8,128)} %collective-permute-done.17.refs_3_, ...), custom_call_target="tpu_custom_call" | custom-call | flops 1024 | bytes 1024 | tf_op jit(solution)/shard_map/mix_band/pallas_call | solution.py:34
  246.8 8.8 %mix_band.13 = (f32[4,256,256]{2,1,0:T(8,128)}, f32[4,256,256]{2,1,0:T(8,128)}) custom-call(f32[8,9]{1,0:T(8,128)} %select_add_fusion.refs_0_, f32[4,512,256]{2,1,0:T(8,128)} %collective-permute-done.16.refs_1_, f32[4,512,256]{2,1,0:T(8,128)} %columns_band.4.rest_0_.refs_1_.refs_2_, f32[4,512,256]{2,1,0:T(8,128)} %columns_band.5.refs_6_.refs_2_.refs_3_, ...), custom_call_target="tpu_custom_call" | custom-call | flops 1024 | bytes 1024 | tf_op jit(solution)/shard_map/mix_band/pallas_call | solution.py:34
  259.8 8.8 %mix_band.14 = (f32[4,256,256]{2,1,0:T(8,128)}, f32[4,256,256]{2,1,0:T(8,128)}) custom-call(f32[8,9]{1,0:T(8,128)} %select_add_fusion.refs_0_, f32[4,512,256]{2,1,0:T(8,128)} %collective-permute-done.15.refs_1_, f32[4,512,256]{2,1,0:T(8,128)} %columns_band.7.refs_6_.refs_2_.refs_1_, f32[4,512,256]{2,1,0:T(8,128)} %columns_band.6.refs_6_.refs_3_.refs_2_, ...), custom_call_target="tpu_custom_call" | custom-call | flops 1024 | bytes 1024 | tf_op jit(solution)/shard_map/mix_band/pallas_call | solution.py:34
  270.0 8.8 %mix_band.15 = (f32[4,256,256]{2,1,0:T(8,128)}, f32[4,256,256]{2,1,0:T(8,128)}) custom-call(f32[8,9]{1,0:T(8,128)} %select_add_fusion.refs_0_, f32[4,512,256]{2,1,0:T(8,128)} %columns_band.7.refs_6_.refs_2_.refs_1_, f32[4,512,256]{2,1,0:T(8,128)} %columns_band.6.refs_6_.refs_3_.refs_2_, f32[4,512,256]{2,1,0:T(8,128)} %copy-done.5, ...), custom_call_target="tpu_custom_call" | custom-call | flops 1024 | bytes 1024 | tf_op jit(solution)/shard_map/mix_band/pallas_call | solution.py:34
  280.7 7.0 %band.3 = (bf16[8,512,512]{2,1,0:T(8,128)(2,1)}, bf16[8,512,512]{2,1,0:T(8,128)(2,1)}) custom-call(s32[2]{0:T(128)} %pad_add_fusion.2.bases, s32[8,1,512]{2,1,0:T(1,128)} %broadcast_in_dim.75.offset, f32[4,8,1,512]{3,2,1,0:T(1,128)} %broadcast_in_dim.76.weight), custom_call_target="tpu_custom_call" | custom-call | flops 1024 | bytes 1024 | tf_op jit(solution)/shard_map/band/pallas_call | solution.py:71
  298.2 16.0 %collective-permute-done.20.refs_3_ = f32[4,256,256]{2,1,0:T(8,128)} collective-permute-done((f32[4,256,256]{2,1,0:T(8,128)}, f32[4,256,256]{2,1,0:T(8,128)}, u32[]{:S(2)}, u32[]{:S(2)}) %collective-permute-start.20) | collective-permute-done | bytes 1048608 | tf_op jit(solution)/shard_map/ppermute | solution.py:271
  314.3 22.9 %collective-permute-done.21.refs_4_ = f32[4,256,256]{2,1,0:T(8,128)} collective-permute-done((f32[4,256,256]{2,1,0:T(8,128)}, f32[4,256,256]{2,1,0:T(8,128)}, u32[]{:S(2)}, u32[]{:S(2)}) %collective-permute-start.21) | collective-permute-done | bytes 1048608 | tf_op jit(solution)/shard_map/ppermute | solution.py:271
  343.2 6.1 %last_rows.6.refs_5_ = f32[2,8,256,512]{3,2,1,0:T(8,128)} custom-call(bf16[8,512,512]{2,1,0:T(8,128)(2,1)} %get-tuple-element.27.refs_0_, bf16[8,512,512]{2,1,0:T(8,128)(2,1)} %get-tuple-element.28.refs_1_, f32[2,8,256,512]{3,2,1,0:T(8,128)} %refs_2_.15, f32[4,256,256]{2,1,0:T(8,128)} %get-tuple-element.43.refs_6_.refs_3_, ...), custom_call_target="tpu_custom_call", output_to_operand_aliasing={{}: (5, {})} | custom-call | flops 1024 | bytes 1024 | tf_op jit(solution)/shard_map/last_rows/pallas_call | solution.py:34
  349.3 10.2 %collective-permute-done.18.refs_4_ = f32[4,256,256]{2,1,0:T(8,128)S(1)} collective-permute-done((f32[4,256,256]{2,1,0:T(8,128)}, f32[4,256,256]{2,1,0:T(8,128)S(1)}, u32[]{:S(2)}, u32[]{:S(2)}) %collective-permute-start.18) | collective-permute-done | bytes 1048608 | tf_op jit(solution)/shard_map/ppermute | solution.py:271
  (99 shorter events, 108.8 us)
Async XLA Ops:
  3.4 24.2 %collective-permute-start.3 = (f32[4,256,256]{2,1,0:T(8,128)}, f32[4,256,256]{2,1,0:T(8,128)S(1)}, u32[]{:S(2)}, u32[]{:S(2)}) collective-permute-start(f32[4,256,256]{2,1,0:T(8,128)} %take.8.rest_0_), channel_id=1, source_target_pairs={{0,16},{1,17},{2,18},{3,19},{16,0},{17,1},{18,2},{19,3},{4,20},{5,... | collective-permute-start | bytes 3145736 | tf_op jit(solution)/shard_map/ppermute | solution.py:271
  11.5 27.2 %collective-permute-start.2 = (f32[4,256,512]{2,1,0:T(8,128)}, f32[4,256,512]{2,1,0:T(8,128)}, u32[]{:S(2)}, u32[]{:S(2)}) collective-permute-start(f32[4,256,512]{2,1,0:T(8,128)} %get-tuple-element.50), channel_id=1, source_target_pairs={{0,4},{4,8},{8,12},{1,5},{5,9},{9,13},{2,6},{6,10},{10,14},{3,7},{... | collective-permute-start | bytes 6291464 | tf_op jit(solution)/shard_map/ppermute | solution.py:263
  15.5 32.5 %collective-permute-start.1 = (f32[4,256,512]{2,1,0:T(8,128)}, f32[4,256,512]{2,1,0:T(8,128)}, u32[]{:S(2)}, u32[]{:S(2)}) collective-permute-start(f32[4,256,512]{2,1,0:T(8,128)} %get-tuple-element.51), channel_id=1, source_target_pairs={{4,0},{8,4},{12,8},{5,1},{9,5},{13,9},{6,2},{10,6},{14,10},{7,3},{... | collective-permute-start | bytes 6291464 | tf_op jit(solution)/shard_map/ppermute | solution.py:263
  17.4 43.8 %collective-permute-start = (f32[4,256,512]{2,1,0:T(8,128)}, f32[4,256,512]{2,1,0:T(8,128)}, u32[]{:S(2)}, u32[]{:S(2)}) collective-permute-start(f32[4,256,512]{2,1,0:T(8,128)} %get-tuple-element.52), channel_id=1, source_target_pairs={{0,4},{4,8},{8,12},{1,5},{5,9},{9,13},{2,6},{6,10},{10,14},{3,7},{... | collective-permute-start | bytes 6291464 | tf_op jit(solution)/shard_map/ppermute | solution.py:263
  21.1 49.0 %collective-permute-start.8 = (f32[4,256,512]{2,1,0:T(8,128)}, f32[4,256,512]{2,1,0:T(8,128)}, u32[]{:S(2)}, u32[]{:S(2)}) collective-permute-start(f32[4,256,512]{2,1,0:T(8,128)} %get-tuple-element.49), channel_id=1, source_target_pairs={{4,0},{8,4},{12,8},{5,1},{9,5},{13,9},{6,2},{10,6},{14,10},{7,3},{... | collective-permute-start | bytes 6291464 | tf_op jit(solution)/shard_map/ppermute | solution.py:263
  27.6 29.3 %collective-permute-start.4 = (f32[4,256,256]{2,1,0:T(8,128)}, f32[4,256,256]{2,1,0:T(8,128)S(1)}, u32[]{:S(2)}, u32[]{:S(2)}) collective-permute-start(f32[4,256,256]{2,1,0:T(8,128)} %take.9), channel_id=1, source_target_pairs={{0,16},{1,17},{2,18},{3,19},{16,0},{17,1},{18,2},{19,3},{4,20},{5,... | collective-permute-start | bytes 3145736 | tf_op jit(solution)/shard_map/ppermute | solution.py:271
  47.7 43.9 %collective-permute-start.7 = (f32[4,256,256]{2,1,0:T(8,128)}, f32[4,256,256]{2,1,0:T(8,128)}, u32[]{:S(2)}, u32[]{:S(2)}) collective-permute-start(f32[4,256,256]{2,1,0:T(8,128)} %get-tuple-element.37), channel_id=1, source_target_pairs={{0,16},{1,17},{2,18},{3,19},{16,0},{17,1},{18,2},{19,3},{4,20},{5,... | collective-permute-start | bytes 3145736 | tf_op jit(solution)/shard_map/ppermute | solution.py:271
  85.9 25.4 %collective-permute-start.12 = (f32[4,256,256]{2,1,0:T(8,128)}, f32[4,256,256]{2,1,0:T(8,128)S(1)}, u32[]{:S(2)}, u32[]{:S(2)}) collective-permute-start(f32[4,256,256]{2,1,0:T(8,128)} %take.12.refs_6_), channel_id=1, source_target_pairs={{0,16},{1,17},{2,18},{3,19},{16,0},{17,1},{18,2},{19,3},{4,20},{5,... | collective-permute-start | bytes 3145736 | tf_op jit(solution)/shard_map/ppermute | solution.py:271
  86.1 46.6 %collective-permute-start.9 = (f32[4,256,256]{2,1,0:T(8,128)}, f32[4,256,256]{2,1,0:T(8,128)S(1)}, u32[]{:S(2)}, u32[]{:S(2)}) collective-permute-start(f32[4,256,256]{2,1,0:T(8,128)} %take.11.rest_0_), channel_id=1, source_target_pairs={{0,16},{1,17},{2,18},{3,19},{16,0},{17,1},{18,2},{19,3},{4,20},{5,... | collective-permute-start | bytes 3145736 | tf_op jit(solution)/shard_map/ppermute | solution.py:271
  87.4 65.4 %collective-permute-start.10 = (f32[4,256,256]{2,1,0:T(8,128)}, f32[4,256,256]{2,1,0:T(8,128)S(1)}, u32[]{:S(2)}, u32[]{:S(2)}) collective-permute-start(f32[4,256,256]{2,1,0:T(8,128)} %get-tuple-element.38.rest_0_), channel_id=1, source_target_pairs={{1,0},{2,1},{3,2},{17,16},{18,17},{19,18},{5,4},{6,5},{7,6},{21,20... | collective-permute-start | bytes 3145736 | tf_op jit(solution)/shard_map/ppermute | solution.py:271
  89.5 72.5 %collective-permute-start.5 = (f32[4,256,256]{2,1,0:T(8,128)}, f32[4,256,256]{2,1,0:T(8,128)}, u32[]{:S(2)}, u32[]{:S(2)}) collective-permute-start(f32[4,256,256]{2,1,0:T(8,128)} %get-tuple-element.35.refs_6_), channel_id=1, source_target_pairs={{1,0},{2,1},{3,2},{17,16},{18,17},{19,18},{5,4},{6,5},{7,6},{21,20... | collective-permute-start | bytes 3145736 | tf_op jit(solution)/shard_map/ppermute | solution.py:271
  91.6 70.4 %collective-permute-start.11 = (f32[4,256,256]{2,1,0:T(8,128)}, f32[4,256,256]{2,1,0:T(8,128)}, u32[]{:S(2)}, u32[]{:S(2)}) collective-permute-start(f32[4,256,256]{2,1,0:T(8,128)} %get-tuple-element.39), channel_id=1, source_target_pairs={{1,16},{2,17},{3,18},{17,0},{18,1},{19,2},{5,20},{6,21},{7,22},{21... | collective-permute-start | bytes 3145736 | tf_op jit(solution)/shard_map/ppermute | solution.py:271
  111.3 70.4 %collective-permute-start.6 = (f32[4,256,256]{2,1,0:T(8,128)}, f32[4,256,256]{2,1,0:T(8,128)}, u32[]{:S(2)}, u32[]{:S(2)}) collective-permute-start(f32[4,256,256]{2,1,0:T(8,128)} %get-tuple-element.36), channel_id=1, source_target_pairs={{1,16},{2,17},{3,18},{17,0},{18,1},{19,2},{5,20},{6,21},{7,22},{21... | collective-permute-start | bytes 3145736 | tf_op jit(solution)/shard_map/ppermute | solution.py:271
  132.8 70.3 %collective-permute-start.13 = (f32[4,256,256]{2,1,0:T(8,128)}, f32[4,256,256]{2,1,0:T(8,128)}, u32[]{:S(2)}, u32[]{:S(2)}) collective-permute-start(f32[4,256,256]{2,1,0:T(8,128)} %get-tuple-element.40), channel_id=1, source_target_pairs={{0,16},{1,17},{2,18},{3,19},{16,0},{17,1},{18,2},{19,3},{4,20},{5,... | collective-permute-start | bytes 3145736 | tf_op jit(solution)/shard_map/ppermute | solution.py:271
  152.8 80.3 %collective-permute-start.17 = (f32[4,512,256]{2,1,0:T(8,128)}, f32[4,512,256]{2,1,0:T(8,128)}, u32[]{:S(2)}, u32[]{:S(2)}) collective-permute-start(f32[4,512,256]{2,1,0:T(8,128)} %columns_band.4.rest_0_.refs_1_.refs_2_), channel_id=1, source_target_pairs={{4,0},{8,4},{12,8},{5,1},{9,5},{13,9},{6,2},{10,6},{14,10},{7,3},{... | collective-permute-start | bytes 6291464 | tf_op jit(solution)/shard_map/ppermute | solution.py:263
  209.2 37.6 %collective-permute-start.16 = (f32[4,512,256]{2,1,0:T(8,128)}, f32[4,512,256]{2,1,0:T(8,128)}, u32[]{:S(2)}, u32[]{:S(2)}) collective-permute-start(f32[4,512,256]{2,1,0:T(8,128)} %columns_band.5.refs_6_.refs_2_.refs_3_), channel_id=1, source_target_pairs={{0,4},{4,8},{8,12},{1,5},{5,9},{9,13},{2,6},{6,10},{10,14},{3,7},{... | collective-permute-start | bytes 6291464 | tf_op jit(solution)/shard_map/ppermute | solution.py:263
  217.3 40.3 %collective-permute-start.15 = (f32[4,512,256]{2,1,0:T(8,128)}, f32[4,512,256]{2,1,0:T(8,128)}, u32[]{:S(2)}, u32[]{:S(2)}) collective-permute-start(f32[4,512,256]{2,1,0:T(8,128)} %columns_band.6.refs_6_.refs_3_.refs_2_), channel_id=1, source_target_pairs={{0,4},{4,8},{8,12},{1,5},{5,9},{9,13},{2,6},{6,10},{10,14},{3,7},{... | collective-permute-start | bytes 6291464 | tf_op jit(solution)/shard_map/ppermute | solution.py:263
  228.7 39.9 %collective-permute-start.14 = (f32[4,512,256]{2,1,0:T(8,128)}, f32[4,512,256]{2,1,0:T(8,128)S(1)}, u32[]{:S(2)}, u32[]{:S(2)}) collective-permute-start(f32[4,512,256]{2,1,0:T(8,128)} %columns_band.7.refs_6_.refs_2_.refs_1_), channel_id=1, source_target_pairs={{4,0},{8,4},{12,8},{5,1},{9,5},{13,9},{6,2},{10,6},{14,10},{7,3},{... | collective-permute-start | bytes 6291464 | tf_op jit(solution)/shard_map/ppermute | solution.py:263
  241.9 36.9 %collective-permute-start.22 = (f32[4,256,256]{2,1,0:T(8,128)}, f32[4,256,256]{2,1,0:T(8,128)S(1)}, u32[]{:S(2)}, u32[]{:S(2)}) collective-permute-start(f32[4,256,256]{2,1,0:T(8,128)} %get-tuple-element.41.refs_6_), channel_id=1, source_target_pairs={{1,0},{2,1},{3,2},{17,16},{18,17},{19,18},{5,4},{6,5},{7,6},{21,20... | collective-permute-start | bytes 3145736 | tf_op jit(solution)/shard_map/ppermute | solution.py:271
  244.0 48.2 %collective-permute-start.23 = (f32[4,256,256]{2,1,0:T(8,128)}, f32[4,256,256]{2,1,0:T(8,128)}, u32[]{:S(2)}, u32[]{:S(2)}) collective-permute-start(f32[4,256,256]{2,1,0:T(8,128)} %get-tuple-element.48), channel_id=1, source_target_pairs={{1,16},{2,17},{3,18},{17,0},{18,1},{19,2},{5,20},{6,21},{7,22},{21... | collective-permute-start | bytes 3145736 | tf_op jit(solution)/shard_map/ppermute | solution.py:271
  255.7 58.6 %collective-permute-start.20 = (f32[4,256,256]{2,1,0:T(8,128)}, f32[4,256,256]{2,1,0:T(8,128)}, u32[]{:S(2)}, u32[]{:S(2)}) collective-permute-start(f32[4,256,256]{2,1,0:T(8,128)} %get-tuple-element.42.refs_6_), channel_id=1, source_target_pairs={{1,0},{2,1},{3,2},{17,16},{18,17},{19,18},{5,4},{6,5},{7,6},{21,20... | collective-permute-start | bytes 3145736 | tf_op jit(solution)/shard_map/ppermute | solution.py:271
  257.6 79.5 %collective-permute-start.21 = (f32[4,256,256]{2,1,0:T(8,128)}, f32[4,256,256]{2,1,0:T(8,128)}, u32[]{:S(2)}, u32[]{:S(2)}) collective-permute-start(f32[4,256,256]{2,1,0:T(8,128)} %get-tuple-element.47), channel_id=1, source_target_pairs={{1,16},{2,17},{3,18},{17,0},{18,1},{19,2},{5,20},{6,21},{7,22},{21... | collective-permute-start | bytes 3145736 | tf_op jit(solution)/shard_map/ppermute | solution.py:271
  268.7 74.6 %collective-permute-start.19 = (f32[4,256,256]{2,1,0:T(8,128)}, f32[4,256,256]{2,1,0:T(8,128)}, u32[]{:S(2)}, u32[]{:S(2)}) collective-permute-start(f32[4,256,256]{2,1,0:T(8,128)} %get-tuple-element.46), channel_id=1, source_target_pairs={{0,16},{1,17},{2,18},{3,19},{16,0},{17,1},{18,2},{19,3},{4,20},{5,... | collective-permute-start | bytes 3145736 | tf_op jit(solution)/shard_map/ppermute | solution.py:271
  278.8 80.7 %collective-permute-start.18 = (f32[4,256,256]{2,1,0:T(8,128)}, f32[4,256,256]{2,1,0:T(8,128)S(1)}, u32[]{:S(2)}, u32[]{:S(2)}) collective-permute-start(f32[4,256,256]{2,1,0:T(8,128)} %get-tuple-element.45), channel_id=1, source_target_pairs={{0,16},{1,17},{2,18},{3,19},{16,0},{17,1},{18,2},{19,3},{4,20},{5,... | collective-permute-start | bytes 3145736 | tf_op jit(solution)/shard_map/ppermute | solution.py:271
  (14 other events, 141.8 us)
